TPU v7x, 32 devices: a whole 2x2x4 slice. The times are simulated.
32 devices in a mesh: rep: 4 (over z), fsdp: 8 (over y, x, core).
Axes of the slice: x: 2, y: 2, z: 4, core: 2. Of those that a mesh axis runs over, the one named last changes fastest.
Arguments:
- tokens: bfloat16 [16384, 640], P(('rep', 'fsdp')), may hold values from -60 to 60
- cotangent: bfloat16 [16384, 640], P(('rep', 'fsdp')), may hold values from -6 to 6
- prefix: int32 [16], replicated, may hold values from 1 to 1023
- w_qkv: bfloat16 [640, 1536], P('fsdp'), may hold values from -0.3043692 to 0.3043692
- w_out: bfloat16 [1024, 640], P('fsdp'), may hold values from -0.2359375 to 0.2359375
- w_gate: bfloat16 [640, 2048], P('fsdp'), may hold values from -0.23321798 to 0.23321798
- w_up: bfloat16 [640, 2048], P('fsdp'), may hold values from -0.23321798 to 0.23321798
- w_down: bfloat16 [2048, 640], P('fsdp'), may hold values from -0.16683301 to 0.16683301
- gains: bfloat16 [640, 4], P('fsdp'), may hold values from 0.4 to 2.5
- moment_qkv: float32 [640, 1536], P('fsdp'), may hold values from -16 to 16
- moment_out: float32 [1024, 640], P('fsdp'), may hold values from -16 to 16
- moment_gate: float32 [640, 2048], P('fsdp'), may hold values from -16 to 16
- moment_up: float32 [640, 2048], P('fsdp'), may hold values from -16 to 16
- moment_down: float32 [2048, 640], P('fsdp'), may hold values from -16 to 16
- gain_first: float32 [640, 4], P('fsdp'), may hold values from -96 to 96
- gain_second: float32 [640, 4], P('fsdp'), may hold values from 819.2 to 3276.8
Outputs:
- output: float32 [16384, 640], P(('rep', 'fsdp'))
- grad_tokens: float32 [16384, 640], P(('rep', 'fsdp'))
- grad_qkv: float32 [640, 1536], P('fsdp')
- grad_out: float32 [1024, 640], P('fsdp')
- grad_gate: float32 [640, 2048], P('fsdp')
- grad_up: float32 [640, 2048], P('fsdp')
- grad_down: float32 [2048, 640], P('fsdp')
- grad_gains: float32 [640, 4], P('fsdp')
- moment_qkv_new: float32 [640, 1536], P('fsdp')
- moment_out_new: float32 [1024, 640], P('fsdp')
- moment_gate_new: float32 [640, 2048], P('fsdp')
- moment_up_new: float32 [640, 2048], P('fsdp')
- moment_down_new: float32 [2048, 640], P('fsdp')
- master_qkv: float32 [640, 1536], P('fsdp')
- master_out: float32 [1024, 640], P('fsdp')
- master_gate: float32 [640, 2048], P('fsdp')
- master_up: float32 [640, 2048], P('fsdp')
- master_down: float32 [2048, 640], P('fsdp')
- first_new: float32 [640, 4], P('fsdp')
- second_new: float32 [640, 4], P('fsdp')
- master_gains: float32 [640, 4], P('fsdp')
- statistics: float32 [4], replicated
All inputs are finite; a program needn't handle non-finite values.
Results may differ from a plain program's by a relative error of at most 0.02.
The roundings to bfloat16 on the way count: a program that leaves them out, or rounds other values in their place, can miss the bound.
Values may be sent and summed in bfloat16 or wider, within the bound.
A program may use at most 256 MiB of HBM per device.

v0:
```python
import jax
import jax.numpy as jnp
from jax import lax
from jax.sharding import PartitionSpec as P

D = 640
HEADS = 4
HEAD_DIM = 256
NS_STEPS = 5
ADAM_STEP = 10


norm_epsilon = 1e-06
soft_cap = 50.0
rotary_base = 10000.0
newton_first = 3.4445
newton_second = -4.775
newton_third = 2.0315
momentum_decay = 0.95
muon_rate = 1.0
first_decay = 0.9
second_decay = 0.95
adam_rate = 1.0
weight_decay = 0.1
adam_epsilon = 1e-08
frobenius_epsilon = 1e-07
masked_score = -1000000000.0


def swapped(x, axis, bit):
    return lax.ppermute(x, axis, [(i, i ^ 1 << bit) for i in range(lax.axis_size(axis))])


def rms_scale(values, gain):
    return (
        values * lax.rsqrt(jnp.mean(values * values, axis=-1, keepdims=True) + norm_epsilon) * gain
    )


def gated_product(gate, upward):
    return (
        0.5
        * gate
        * (1.0 + jnp.tanh(0.7978845608028654 * (gate + 0.044715 * gate * gate * gate)))
        * upward
    )


def rotary_tables(positions, head_dim):
    half_dim = head_dim // 2
    frequency = rotary_base ** (-(jnp.arange(half_dim, dtype=jnp.float32) * 2.0 / head_dim))
    angles = positions.astype(jnp.float32)[:, None] * frequency[None, :]
    return (jnp.cos(angles), jnp.sin(angles))


def rotary(values, cosine, sine):
    half_dim = values.shape[-1] // 2
    first_half = values[..., :half_dim]
    second_half = values[..., half_dim:]
    return jnp.concatenate(
        [first_half * cosine - second_half * sine, second_half * cosine + first_half * sine],
        axis=-1,
    )


def orthogonalize(matrix):
    highest = lax.Precision.HIGHEST
    row_count, col_count = matrix.shape
    frobenius = jnp.sqrt(jnp.sum(matrix * matrix))
    current = matrix / (frobenius + frobenius_epsilon)
    if row_count > col_count:
        current = current.T
    for repeat_number in range(NS_STEPS):
        gram = jnp.dot(current, current.T, precision=highest, preferred_element_type=jnp.float32)
        squared = jnp.dot(gram, gram, precision=highest, preferred_element_type=jnp.float32)
        mixer = newton_second * gram + newton_third * squared
        current = newton_first * current + jnp.dot(
            mixer, current, precision=highest, preferred_element_type=jnp.float32
        )
    if row_count > col_count:
        current = current.T
    return current


def blank(matrix):
    return jnp.zeros_like(matrix)


def shards(
    tokens,
    cotangent,
    prefix,
    w_qkv,
    w_out,
    w_gate,
    w_up,
    w_down,
    gains,
    moment_qkv,
    moment_out,
    moment_gate,
    moment_up,
    moment_down,
    gain_first,
    gain_second,
):
    row_count = tokens.shape[0]
    fsdp_size = lax.axis_size("fsdp")
    fsdp_place = lax.axis_index("fsdp")
    rep_place = lax.axis_index("rep")
    owner_list = [number * fsdp_size // 5 for number in range(5)]
    parity = fsdp_place % 2
    sequence_id = (rep_place * fsdp_size + fsdp_place) // 2
    table_ids = jnp.arange(prefix.shape[0], dtype=jnp.int32)
    prefix_len = jnp.sum(jnp.where(table_ids == sequence_id, prefix, 0))
    positions = parity * row_count + jnp.arange(row_count, dtype=jnp.int32)
    key_positions = jnp.arange(2 * row_count, dtype=jnp.int32)
    score_scale = HEAD_DIM ** (-0.5)
    attn_width = HEADS * HEAD_DIM
    qkv_whole, out_whole, gains_low = (
        lax.all_gather(w_qkv, "fsdp", axis=0, tiled=True),
        lax.all_gather(w_out, "fsdp", axis=0, tiled=True),
        lax.all_gather(gains, "fsdp", axis=0, tiled=True),
    )
    gate_whole, up_whole, down_whole = (
        lax.all_gather(w_gate, "fsdp", axis=0, tiled=True),
        lax.all_gather(w_up, "fsdp", axis=0, tiled=True),
        lax.all_gather(w_down, "fsdp", axis=0, tiled=True),
    )
    gains_whole = gains_low.astype(jnp.float32)
    residual = tokens.astype(jnp.float32)
    normed_one, norm_one_back = jax.vjp(rms_scale, residual, gains_whole[:, 0])
    normed_one_low = normed_one.astype(jnp.bfloat16)
    projected = jnp.dot(normed_one_low, qkv_whole, preferred_element_type=jnp.float32)
    cosine, sine = rotary_tables(positions, HEAD_DIM)
    queries = rotary(
        projected[:, :attn_width].reshape(row_count, HEADS, HEAD_DIM),
        cosine[:, None, :],
        sine[:, None, :],
    ).astype(jnp.bfloat16)
    own_keys = rotary(projected[:, attn_width : attn_width + HEAD_DIM], cosine, sine).astype(
        jnp.bfloat16
    )
    own_values = projected[:, attn_width + HEAD_DIM :].astype(jnp.bfloat16)
    other_keys, other_values = swapped((own_keys, own_values), "fsdp", 0)
    leading = parity == 0
    all_keys = jnp.where(
        leading,
        jnp.concatenate([own_keys, other_keys], axis=0),
        jnp.concatenate([other_keys, own_keys], axis=0),
    )
    all_values = jnp.where(
        leading,
        jnp.concatenate([own_values, other_values], axis=0),
        jnp.concatenate([other_values, own_values], axis=0),
    )
    raw_scores = jnp.einsum("rhd,kd->hrk", queries, all_keys, preferred_element_type=jnp.float32)
    bent_scores = jnp.tanh(raw_scores * score_scale / soft_cap)
    capped = soft_cap * bent_scores
    allowed = (key_positions[None, :] <= positions[:, None]) | (key_positions[None, :] < prefix_len)
    capped = jnp.where(allowed[None], capped, masked_score)
    top_score = jnp.max(capped, axis=-1, keepdims=True)
    weights_exp = jnp.exp(capped - top_score)
    softmaxed = weights_exp / jnp.sum(weights_exp, axis=-1, keepdims=True)
    softmaxed_low = softmaxed.astype(jnp.bfloat16)
    attended = jnp.einsum(
        "hrk,kd->rhd", softmaxed_low, all_values, preferred_element_type=jnp.float32
    )
    attended = attended.reshape(row_count, attn_width).astype(jnp.bfloat16)
    branch_one = jnp.dot(attended, out_whole, preferred_element_type=jnp.float32)
    first_out, first_back = jax.vjp(rms_scale, branch_one, gains_whole[:, 1])
    hidden = residual + first_out
    normed_two, norm_two_back = jax.vjp(rms_scale, hidden, gains_whole[:, 2])
    normed_two_low = normed_two.astype(jnp.bfloat16)
    gate = jnp.dot(normed_two_low, gate_whole, preferred_element_type=jnp.float32)
    upward = jnp.dot(normed_two_low, up_whole, preferred_element_type=jnp.float32)
    active, active_back = jax.vjp(gated_product, gate, upward)
    active_low = active.astype(jnp.bfloat16)
    branch_two = jnp.dot(active_low, down_whole, preferred_element_type=jnp.float32)
    second_out, second_back = jax.vjp(rms_scale, branch_two, gains_whole[:, 3])
    final = hidden + second_out
    valid = (positions >= prefix_len).astype(jnp.float32)
    squares = jnp.stack(
        [
            jnp.sum(valid * jnp.sum(stream * stream, axis=-1))
            for stream in (residual, first_out, second_out, final)
        ]
    )
    total_squares, total_count = lax.psum((squares, jnp.sum(valid)), ("rep", "fsdp"))
    statistics = jnp.sqrt(total_squares / (total_count * D))
    qkv_back, out_back = (
        lax.all_gather(w_qkv, "fsdp", axis=0, tiled=True),
        lax.all_gather(w_out, "fsdp", axis=0, tiled=True),
    )
    gate_back, up_back, down_back = (
        lax.all_gather(w_gate, "fsdp", axis=0, tiled=True),
        lax.all_gather(w_up, "fsdp", axis=0, tiled=True),
        lax.all_gather(w_down, "fsdp", axis=0, tiled=True),
    )
    upstream = cotangent.astype(jnp.float32)
    d_branch_two, d_gain_three = second_back(upstream)
    d_branch_two_low = d_branch_two.astype(jnp.bfloat16)
    grad_down_part = jnp.einsum(
        "rf,rd->fd", active_low, d_branch_two_low, preferred_element_type=jnp.float32
    )
    d_active = jnp.einsum(
        "rd,fd->rf", d_branch_two_low, down_back, preferred_element_type=jnp.float32
    )
    d_gate, d_upward = active_back(d_active)
    d_gate_low = d_gate.astype(jnp.bfloat16)
    d_upward_low = d_upward.astype(jnp.bfloat16)
    grad_gate_part = jnp.einsum(
        "rd,rf->df", normed_two_low, d_gate_low, preferred_element_type=jnp.float32
    )
    grad_up_part = jnp.einsum(
        "rd,rf->df", normed_two_low, d_upward_low, preferred_element_type=jnp.float32
    )
    d_normed_two = jnp.einsum(
        "rf,df->rd", d_gate_low, gate_back, preferred_element_type=jnp.float32
    ) + jnp.einsum("rf,df->rd", d_upward_low, up_back, preferred_element_type=jnp.float32)
    d_hidden_norm, d_gain_two = norm_two_back(d_normed_two)
    d_hidden = upstream + d_hidden_norm
    d_branch_one, d_gain_one = first_back(d_hidden)
    d_branch_one_low = d_branch_one.astype(jnp.bfloat16)
    grad_out_part = jnp.einsum(
        "ra,rd->ad", attended, d_branch_one_low, preferred_element_type=jnp.float32
    )
    d_attended = jnp.einsum(
        "rd,ad->ra", d_branch_one_low, out_back, preferred_element_type=jnp.float32
    )
    d_attended = d_attended.astype(jnp.bfloat16).reshape(row_count, HEADS, HEAD_DIM)
    d_soft = jnp.einsum("rhd,kd->hrk", d_attended, all_values, preferred_element_type=jnp.float32)
    d_values_all = jnp.einsum(
        "hrk,rhd->kd", softmaxed_low, d_attended, preferred_element_type=jnp.float32
    )
    d_capped = softmaxed * (d_soft - jnp.sum(d_soft * softmaxed, axis=-1, keepdims=True))
    d_raw = (d_capped * (1.0 - bent_scores * bent_scores) * score_scale).astype(jnp.bfloat16)
    d_queries = jnp.einsum("hrk,kd->rhd", d_raw, all_keys, preferred_element_type=jnp.float32)
    d_keys_all = jnp.einsum("hrk,rhd->kd", d_raw, queries, preferred_element_type=jnp.float32)
    own_start = parity * row_count
    other_start = (1 - parity) * row_count
    returned_keys, returned_values = (
        swapped(
            lax.dynamic_slice_in_dim(d_keys_all, other_start, row_count, 0).astype(jnp.bfloat16),
            "fsdp",
            0,
        ).astype(jnp.float32),
        swapped(
            lax.dynamic_slice_in_dim(d_values_all, other_start, row_count, 0).astype(jnp.bfloat16),
            "fsdp",
            0,
        ).astype(jnp.float32),
    )
    d_keys = lax.dynamic_slice_in_dim(d_keys_all, own_start, row_count, 0) + returned_keys
    d_values = lax.dynamic_slice_in_dim(d_values_all, own_start, row_count, 0) + returned_values
    d_projected = jnp.concatenate(
        [
            rotary(d_queries, cosine[:, None, :], -sine[:, None, :]).reshape(row_count, attn_width),
            rotary(d_keys, cosine, -sine),
            d_values,
        ],
        axis=1,
    ).astype(jnp.bfloat16)
    grad_qkv_part = jnp.einsum(
        "rd,re->de", normed_one_low, d_projected, preferred_element_type=jnp.float32
    )
    d_normed_one = jnp.einsum(
        "re,de->rd", d_projected, qkv_back, preferred_element_type=jnp.float32
    )
    d_residual_norm, d_gain_zero = norm_one_back(d_normed_one)
    grad_tokens = d_hidden + d_residual_norm
    grad_gains_part = jnp.stack([d_gain_zero, d_gain_one, d_gain_two, d_gain_three], axis=1)
    reduced = (
        lax.psum_scatter(grad_qkv_part, "fsdp", scatter_dimension=0, tiled=True),
        lax.psum_scatter(grad_out_part, "fsdp", scatter_dimension=0, tiled=True),
        lax.psum_scatter(grad_gate_part, "fsdp", scatter_dimension=0, tiled=True),
        lax.psum_scatter(grad_up_part, "fsdp", scatter_dimension=0, tiled=True),
        lax.psum_scatter(grad_down_part, "fsdp", scatter_dimension=0, tiled=True),
        lax.psum_scatter(grad_gains_part, "fsdp", scatter_dimension=0, tiled=True),
    )
    reduced = lax.psum(
        (reduced[0], reduced[1], reduced[2], reduced[3], reduced[4], reduced[5]), "rep"
    )
    moments = (moment_qkv, moment_out, moment_gate, moment_up, moment_down)
    weight_shards = (w_qkv, w_out, w_gate, w_up, w_down)
    full_shapes = [(shard.shape[0] * fsdp_size, shard.shape[1]) for shard in weight_shards]
    new_moments = tuple(
        (
            momentum_decay * moments[number] + (1.0 - momentum_decay) * reduced[number]
            for number in range(5)
        )
    )
    nesterov = tuple(
        (
            (1.0 - momentum_decay) * reduced[number] + momentum_decay * new_moments[number]
            for number in range(5)
        )
    )
    gathered = (
        lax.all_gather(nesterov[0], "fsdp", axis=0, tiled=True),
        lax.all_gather(nesterov[1], "fsdp", axis=0, tiled=True),
        lax.all_gather(nesterov[2], "fsdp", axis=0, tiled=True),
        lax.all_gather(nesterov[3], "fsdp", axis=0, tiled=True),
        lax.all_gather(nesterov[4], "fsdp", axis=0, tiled=True),
    )
    results = tuple(
        (
            lax.cond(fsdp_place == owner_list[number], orthogonalize, blank, gathered[number])
            for number in range(5)
        )
    )
    ortho_shards = (
        lax.psum_scatter(
            results[0].astype(jnp.bfloat16), "fsdp", scatter_dimension=0, tiled=True
        ).astype(jnp.float32),
        lax.psum_scatter(
            results[1].astype(jnp.bfloat16), "fsdp", scatter_dimension=0, tiled=True
        ).astype(jnp.float32),
        lax.psum_scatter(
            results[2].astype(jnp.bfloat16), "fsdp", scatter_dimension=0, tiled=True
        ).astype(jnp.float32),
        lax.psum_scatter(
            results[3].astype(jnp.bfloat16), "fsdp", scatter_dimension=0, tiled=True
        ).astype(jnp.float32),
        lax.psum_scatter(
            results[4].astype(jnp.bfloat16), "fsdp", scatter_dimension=0, tiled=True
        ).astype(jnp.float32),
    )
    masters = tuple(
        (
            weight_shards[number].astype(jnp.float32)
            - muon_rate
            * max(1.0, full_shapes[number][0] / full_shapes[number][1]) ** 0.5
            * ortho_shards[number]
            for number in range(5)
        )
    )
    gain_grad = reduced[5]
    gains_local = gains.astype(jnp.float32)
    first_new = first_decay * gain_first + (1.0 - first_decay) * gain_grad
    second_new = second_decay * gain_second + (1.0 - second_decay) * gain_grad * gain_grad
    first_hat = first_new / (1.0 - first_decay**ADAM_STEP)
    second_hat = second_new / (1.0 - second_decay**ADAM_STEP)
    master_gains = gains_local - adam_rate * (
        first_hat / (jnp.sqrt(second_hat) + adam_epsilon) + weight_decay * gains_local
    )
    return (
        final,
        grad_tokens,
        reduced[0],
        reduced[1],
        reduced[2],
        reduced[3],
        reduced[4],
        gain_grad,
        new_moments[0],
        new_moments[1],
        new_moments[2],
        new_moments[3],
        new_moments[4],
        masters[0],
        masters[1],
        masters[2],
        masters[3],
        masters[4],
        first_new,
        second_new,
        master_gains,
        statistics,
    )


def solution(mesh):
    in_specs = (
        P(("rep", "fsdp"), None),
        P(("rep", "fsdp"), None),
        P(),
        P("fsdp", None),
        P("fsdp", None),
        P("fsdp", None),
        P("fsdp", None),
        P("fsdp", None),
        P("fsdp", None),
        P("fsdp", None),
        P("fsdp", None),
        P("fsdp", None),
        P("fsdp", None),
        P("fsdp", None),
        P("fsdp", None),
        P("fsdp", None),
    )
    out_specs = (
        P(("rep", "fsdp"), None),
        P(("rep", "fsdp"), None),
        P("fsdp", None),
        P("fsdp", None),
        P("fsdp", None),
        P("fsdp", None),
        P("fsdp", None),
        P("fsdp", None),
        P("fsdp", None),
        P("fsdp", None),
        P("fsdp", None),
        P("fsdp", None),
        P("fsdp", None),
        P("fsdp", None),
        P("fsdp", None),
        P("fsdp", None),
        P("fsdp", None),
        P("fsdp", None),
        P("fsdp", None),
        P("fsdp", None),
        P("fsdp", None),
        P(),
    )
    return jax.shard_map(shards, mesh=mesh, in_specs=in_specs, out_specs=out_specs, check_vma=False)
```

profile of v0, /device:TPU:0, one launch (start us, length us, event | category | flops | bytes accessed | tf_op | source)
XLA Modules:
  0.0 1071.8 jit_solution(3576759178512448811)
XLA Ops:
  11.2 10.5 all-gather
  25.7 14.3 %all-gather.12.cloned.1.call-done = bf16[640,1536]{1,0:T(8,128)(2,1)} async-done(((bf16[80,1536]{1,0:T(8,128)(2,1)}), bf16[640,1536]{1,0:T(8,128)(2,1)}) %all-gather.12.cloned.1.call-update) | async-done | bytes 1966096 | tf_op jit(solution)/shard_map/all_gather | solution.py:121
  54.4 5.1 fusion.310
  70.7 27.8 %all-gather.16.cloned.1.call-done = bf16[640,2048]{1,0:T(8,128)(2,1)} async-done(((bf16[80,2048]{1,0:T(8,128)(2,1)}), bf16[640,2048]{1,0:T(8,128)(2,1)}) %all-gather.16.cloned.1.call-update) | async-done | bytes 2621456 | tf_op jit(solution)/shard_map/all_gather | solution.py:126
  98.6 5.5 fusion.350
  104.1 26.4 %all-gather.18.cloned.1.call-done = bf16[640,2048]{1,0:T(8,128)(2,1)} async-done(((bf16[80,2048]{1,0:T(8,128)(2,1)}), bf16[640,2048]{1,0:T(8,128)(2,1)}) %all-gather.18.cloned.1.call-update) | async-done | bytes 2621456 | tf_op jit(solution)/shard_map/all_gather | solution.py:127
  130.5 6.7 multiply_convert_fusion.1
  137.1 25.2 %all-gather.20.cloned.1.call-done = bf16[2048,640]{1,0:T(8,128)(2,1)} async-done(((bf16[256,640]{1,0:T(8,128)(2,1)}), bf16[2048,640]{1,0:T(8,128)(2,1)}) %all-gather.20.cloned.1.call-update) | async-done | bytes 2621456 | tf_op jit(solution)/shard_map/all_gather | solution.py:128
  162.3 4.4 multiply_reduce_fusion.12
  170.4 5.8 multiply_convert_fusion
  191.2 4.6 fusion.260
  195.8 19.3 %fusion.240 = f32[1024,256]{1,0:T(8,128)} fusion(f32[1024,512,4]{1,0,2:T(8,128)} %fusion.260, f32[1024,512,4]{1,0,2:T(8,128)} %copy-done.3, bf16[512,4,128]{2,0,1:T(8,128)(2,1)S(1)} %copy-done.27, bf16[512,4,128]{2,0,1:T(8,128)(2,1)S(1)} %copy-done.25, f32[4,512,1024]{1,2,0:T(8,128)} %copy-done.96, f32[4,512]{1,0:T(4,128)S(1)} %copy-done.98), kind=kOutput, calls=%fused_computation.308 | convolution fusion | flops 1098910720 | bytes 27271168 | tf_op jit(solution)/shard_map/hrk,rhd->kd/dot_general | solution.py:239
  217.3 17.0 %fusion.232 = f32[512,4,256]{2,0,1:T(8,128)} fusion(f32[1024,512,4]{1,0,2:T(8,128)} %fusion.260, f32[1024,512,4]{1,0,2:T(8,128)} %copy-done.3, bf16[512,256]{1,0:T(8,128)(2,1)S(1)} %copy-done.55, bf16[512,128]{1,0:T(8,128)(2,1)S(1)} %copy-done.37, bf16[512,128]{1,0:T(8,128)(2,1)S(1)} %copy-done.39, pred[]{:T(512)S(6)} %eq.26, ...), kind=kOutput, calls=%fused_computation.300 | convolution fusion | flops 1100221440 | bytes 27795456 | tf_op jit(solution)/shard_map/hrk,kd->rhd/dot_general | solution.py:238
  234.3 5.8 fusion.241
  251.2 5.8 fusion.355
  257.1 5.8 fusion.354
  263.3 5.5 fusion.353
  268.9 31.6 %reduce-scatter.14.cloned.1.call-done = f32[80,1536]{1,0:T(8,128)} async-done(((f32[640,1536]{1,0:T(8,128)}), f32[80,1536]{1,0:T(8,128)}) %reduce-scatter.14.cloned.1.call-update) | async-done | bytes 491536 | tf_op jit(solution)/shard_map/reduce_scatter | solution.py:274
  300.6 60.4 %reduce-scatter.22.cloned.1.call-done = f32[256,640]{1,0:T(8,128)} async-done(((f32[2048,640]{1,0:T(8,128)}), f32[256,640]{1,0:T(8,128)}) %reduce-scatter.22.cloned.1.call-update) | async-done | bytes 655376 | tf_op jit(solution)/shard_map/reduce_scatter | solution.py:278
  360.9 60.0 %reduce-scatter.20.cloned.1.call-done = f32[80,2048]{1,0:T(8,128)} async-done(((f32[640,2048]{1,0:T(8,128)}), f32[80,2048]{1,0:T(8,128)}) %reduce-scatter.20.cloned.1.call-update) | async-done | bytes 655376 | tf_op jit(solution)/shard_map/reduce_scatter | solution.py:277
  420.9 60.2 %reduce-scatter.18.cloned.1.call-done = f32[80,2048]{1,0:T(8,128)} async-done(((f32[640,2048]{1,0:T(8,128)}), f32[80,2048]{1,0:T(8,128)}) %reduce-scatter.18.cloned.1.call-update) | async-done | bytes 655376 | tf_op jit(solution)/shard_map/reduce_scatter | solution.py:276
  481.2 113.6 %all-reduce.4.cloned.1.call-done = (f32[80,1536]{1,0:T(8,128)}, f32[128,640]{1,0:T(8,128)}, f32[80,2048]{1,0:T(8,128)}, f32[80,2048]{1,0:T(8,128)}, f32[256,640]{1,0:T(8,128)}) async-done(((f32[80,1536]{1,0:T(8,128)}, f32[128,640]{1,0:T(8,128)}, f32[80,2048]{1,0:T(8,128)}, f32[80,2048]{1,0:T(8,128)}, f32[256,640]{1,0:T(8,128)}), (f32[80,1536]{1,0:T(8,128)}, f32[128,640]{1,0:T(8,128)}, f32[80,2048]{1,0:T(8,128)}, ...) | async-done | bytes 2785296 | tf_op jit(solution)/shard_map/psum | solution.py:281
  604.5 4.8 fusion.245
  610.2 16.0 %all-gather.24.cloned.1.call-done = f32[1024,640]{1,0:T(8,128)} async-done(((f32[128,640]{1,0:T(8,128)}), f32[1024,640]{1,0:T(8,128)}) %all-gather.24.cloned.1.call-update) | async-done | bytes 2621456 | tf_op jit(solution)/shard_map/all_gather | solution.py:301
  626.2 5.7 conditional.6
  634.5 30.0 %all-gather.22.cloned.1.call-done = f32[640,1536]{1,0:T(8,128)} async-done(((f32[80,1536]{1,0:T(8,128)}), f32[640,1536]{1,0:T(8,128)}) %all-gather.22.cloned.1.call-update) | async-done | bytes 3932176 | tf_op jit(solution)/shard_map/all_gather | solution.py:300
  664.5 127.8 %conditional.5 = (bf16[640,1536]{1,0:T(8,128)(2,1)S(1)}) conditional(s32[]{:T(128)} %convert_element_type.159, () %tuple.38, f32[640,1536]{1,0:T(8,128)} %all-gather.22.cloned.1.call-done), branch_computations={%region_28.29_spmd, %region_29.31_spmd} | conditional | flops 91247984640 | bytes 117637192 | solution.py:308
  668.9 12.3 %fusion.15 = f32[640,640]{1,0:T(8,128)S(1)} fusion(f32[640,1536]{1,0:T(8,128)} %param.1, f32[]{:T(128)S(6)} %add.282), kind=kOutput, calls=%fused_computation.22 | convolution fusion | flops 7550730240 | bytes 5570564 | tf_op jit(solution)/shard_map/cond/branch_1_fun/dot_general | solution.py:74
  681.3 4.6 fusion.311
  685.8 9.7 multiply_add_fusion.4
  695.6 9.5 fusion.312
  705.1 4.8 fusion.313
  709.9 9.5 multiply_add_fusion.3
  719.4 9.9 fusion.314
  729.4 4.7 fusion.315
  734.1 9.5 multiply_add_fusion.2
  743.7 9.8 fusion.316
  753.4 4.6 fusion.317
  758.0 9.9 multiply_add_fusion.1
  767.9 9.7 fusion.318
  777.7 4.6 fusion.319
  782.2 9.7 multiply_add_fusion
  793.7 12.6 %conditional.9 = (bf16[2048,640]{0,1:T(8,128)(2,1)}) conditional(s32[]{:T(128)} %convert_element_type.175, () %tuple.42, f32[2048,640]{1,0:T(8,128)} %all-gather.30.cloned.1.call-done), branch_computations={%region_44.45_spmd, %region_45.47_spmd} | conditional | flops 116449198080 | bytes 295239872 | solution.py:308
  810.9 9.5 conditional.8
  822.1 9.1 conditional.7
  835.8 168.7 %all-reduce = (f32[4]{0:T(128)S(1)}, f32[]{:T(128)}) all-reduce(f32[4]{0:T(128)S(1)} %pad_maximum_fusion.9, f32[]{:T(128)} %get-tuple-element.56), channel_id=1, replica_groups=mesh['rep'=4,'fsdp'=8] {'rep','fsdp'}, use_global_device_ids=true, to_apply=%region_55.56 | all-reduce | flops 5 | bytes 40 | tf_op jit(solution)/shard_map/psum | solution.py:189
  1009.4 10.9 %psum.61 = f32[80,4]{0,1:T(4,128)S(1)} all-reduce(f32[80,4]{0,1:T(4,128)S(1)} %copy.147), channel_id=1, replica_groups=mesh['rep'=4,'fsdp'=8] {'rep'}, use_global_device_ids=true, to_apply=%region_27.28 | all-reduce | flops 320 | bytes 2560 | tf_op jit(solution)/shard_map/psum | solution.py:281
  1028.5 30.2 %reduce-scatter.28.cloned.1.call-done = bf16[80,2048]{1,0:T(8,128)(2,1)} async-done(((bf16[640,2048]{1,0:T(8,128)(2,1)}), bf16[80,2048]{1,0:T(8,128)(2,1)}) %reduce-scatter.28.cloned.1.call-update) | async-done | bytes 327696 | tf_op jit(solution)/shard_map/reduce_scatter | solution.py:319
  (336 shorter events, 117.8 us)
Async XLA Ops:
  7.2 32.8 %copy-start.9 = (bf16[512,640]{1,0:T(8,128)(2,1)S(1)}, bf16[512,640]{1,0:T(8,128)(2,1)}, u32[]{:S(2)}) copy-start(bf16[512,640]{1,0:T(8,128)(2,1)} %param.26) | copy-start | bytes 1966084
  7.2 32.8 %all-gather.12.cloned.1.call-start = ((), (), s32[]{:S(2)}) async-start(), calls=%async_computation.11 | async-start | bytes 2211840 | tf_op jit(solution)/shard_map/all_gather | solution.py:121
  7.9 58.6 %all-gather.14.cloned.1.call-start = ((), (), s32[]{:S(2)}) async-start(), calls=%async_computation.12 | async-start | bytes 1474560 | tf_op jit(solution)/shard_map/all_gather | solution.py:122
  8.7 89.9 %all-gather.16.cloned.1.call-start = ((), (), s32[]{:S(2)}) async-start(), calls=%async_computation.13 | async-start | bytes 2949120 | tf_op jit(solution)/shard_map/all_gather | solution.py:126
  9.4 121.0 %all-gather.18.cloned.1.call-start = ((), (), s32[]{:S(2)}) async-start(), calls=%async_computation.14 | async-start | bytes 2949120 | tf_op jit(solution)/shard_map/all_gather | solution.py:127
  10.0 152.3 %all-gather.20.cloned.1.call-start = ((), (), s32[]{:S(2)}) async-start(), calls=%async_computation.15 | async-start | bytes 2949120 | tf_op jit(solution)/shard_map/all_gather | solution.py:128
  10.6 258.3 %reduce-scatter.16.cloned.1.call-start = ((), (), s32[]{:S(2)}) async-start(), calls=%async_computation.17 | async-start | bytes 2949120 | tf_op jit(solution)/shard_map/reduce_scatter | solution.py:275
  11.2 36.9 %copy-start.60 = (f32[512]{0:T(512)}, f32[512]{0:T(512)S(1)}, u32[]{:S(2)}) copy-start(f32[512]{0:T(512)S(1)} %fusion.285) | copy-start | bytes 6148
  21.8 21.2 %copy-start.70 = (f32[640]{0:T(1024)}, f32[640]{0:T(1024)S(1)}, u32[]{:S(2)}) copy-start(f32[640]{0:T(1024)S(1)} %get-tuple-element.55) | copy-start | bytes 7684
  23.1 19.9 %copy-start.66 = (f32[512]{0:T(512)}, f32[512]{0:T(512)S(1)}, u32[]{:S(2)}) copy-start(f32[512]{0:T(512)S(1)} %fusion.251) | copy-start | bytes 6148
  23.1 19.9 %copy-start.73 = (f32[512]{0:T(512)}, f32[512]{0:T(512)S(1)}, u32[]{:S(2)}) copy-start(f32[512]{0:T(512)S(1)} %fusion.283) | copy-start | bytes 6148
  51.2 1.6 collective-permute-start.1
  51.6 8.0 collective-permute-start
  190.8 109.8 %reduce-scatter.14.cloned.1.call-start = ((), (), s32[]{:S(2)}) async-start(), calls=%async_computation.16 | async-start | bytes 4423680 | tf_op jit(solution)/shard_map/reduce_scatter | solution.py:274
  195.8 21.5 %copy-start.37 = (bf16[512,128]{1,0:T(8,128)(2,1)S(1)}, bf16[512,128]{1,0:T(8,128)(2,1)}, u32[]{:S(2)}) copy-start(bf16[512,128]{1,0:T(8,128)(2,1)} %copy-done.36) | copy-start | bytes 393220
  195.8 21.5 %copy-start.39 = (bf16[512,128]{1,0:T(8,128)(2,1)S(1)}, bf16[512,128]{1,0:T(8,128)(2,1)}, u32[]{:S(2)}) copy-start(bf16[512,128]{1,0:T(8,128)(2,1)} %copy-done.38) | copy-start | bytes 393220
  195.8 21.5 %copy-start.55 = (bf16[512,256]{1,0:T(8,128)(2,1)S(1)}, bf16[512,256]{1,0:T(8,128)(2,1)}, u32[]{:S(2)}) copy-start(bf16[512,256]{1,0:T(8,128)(2,1)} %copy-done.54) | copy-start | bytes 786436
  216.9 26.0 %collective-permute-start.2 = (bf16[512,256]{1,0:T(8,128)(2,1)}, bf16[512,256]{1,0:T(8,128)(2,1)}, u32[]{:S(2)}, u32[]{:S(2)}) collective-permute-start(bf16[512,256]{1,0:T(8,128)(2,1)} %dynamic-slice_convert_fusion.1), channel_id=1, source_target_pairs={{0,1},{1,0},{2,3},{3,2},{4,5},{5,4},{6,7},{7,6},{8,9},{9,8},{10,11... | collective-permute-start | bytes 786440 | tf_op jit(solution)/shard_map/ppermute | solution.py:31
  242.7 2.9 collective-permute-start.3
  250.2 110.8 %reduce-scatter.22.cloned.1.call-start = ((), (), s32[]{:S(2)}) async-start(), calls=%async_computation.20 | async-start | bytes 5898240 | tf_op jit(solution)/shard_map/reduce_scatter | solution.py:278
  257.0 163.9 %reduce-scatter.20.cloned.1.call-start = ((), (), s32[]{:S(2)}) async-start(), calls=%async_computation.19 | async-start | bytes 5898240 | tf_op jit(solution)/shard_map/reduce_scatter | solution.py:277
  262.9 218.2 %reduce-scatter.18.cloned.1.call-start = ((), (), s32[]{:S(2)}) async-start(), calls=%async_computation.18 | async-start | bytes 5898240 | tf_op jit(solution)/shard_map/reduce_scatter | solution.py:276
  268.9 325.9 %copy-start.51 = (f32[128,640]{1,0:T(8,128)S(1)}, f32[128,640]{1,0:T(8,128)}, u32[]{:S(2)}) copy-start(f32[128,640]{1,0:T(8,128)} %param.36) | copy-start | bytes 983044
  268.9 325.9 %all-reduce.4.cloned.1.call-start = ((), (), s32[]{:S(2)}) async-start(), calls=%async_computation.32 | async-start | bytes 5570560 | tf_op jit(solution)/shard_map/psum | solution.py:281
  481.1 115.7 %copy-start.50 = (f32[80,1536]{1,0:T(8,128)S(1)}, f32[80,1536]{1,0:T(8,128)}, u32[]{:S(2)}) copy-start(f32[80,1536]{1,0:T(8,128)} %param.35) | copy-start | bytes 1474564
  481.1 117.8 %copy-start.46 = (f32[256,640]{1,0:T(8,128)S(1)}, f32[256,640]{1,0:T(8,128)}, u32[]{:S(2)}) copy-start(f32[256,640]{1,0:T(8,128)} %param.39) | copy-start | bytes 1966084
  481.1 145.1 %all-gather.24.cloned.1.call-start = ((), (), s32[]{:S(2)}) async-start(), calls=%async_computation.23 | async-start | bytes 2949120 | tf_op jit(solution)/shard_map/all_gather | solution.py:301
  596.7 67.8 %all-gather.22.cloned.1.call-start = ((), (), s32[]{:S(2)}) async-start(), calls=%async_computation.21 | async-start | bytes 4423680 | tf_op jit(solution)/shard_map/all_gather | solution.py:300
  598.9 194.8 %all-gather.30.cloned.1.call-start = ((), (), s32[]{:S(2)}) async-start(), calls=%async_computation.29 | async-start | bytes 5898240 | tf_op jit(solution)/shard_map/all_gather | solution.py:304
  600.2 210.6 %all-gather.28.cloned.1.call-start = ((), (), s32[]{:S(2)}) async-start(), calls=%async_computation.27 | async-start | bytes 5898240 | tf_op jit(solution)/shard_map/all_gather | solution.py:303
  601.8 220.3 %all-gather.26.cloned.1.call-start = ((), (), s32[]{:S(2)}) async-start(), calls=%async_computation.25 | async-start | bytes 5898240 | tf_op jit(solution)/shard_map/all_gather | solution.py:302
  604.3 404.2 %reduce-scatter.34.cloned.1.call-start = ((), (), s32[]{:S(2)}) async-start(), calls=%async_computation.31 | async-start | bytes 368640
  610.2 410.8 %reduce-scatter.26.cloned.1.call-start = ((), (), s32[]{:S(2)}) async-start(), calls=%async_computation.24 | async-start | bytes 1474560 | tf_op jit(solution)/shard_map/reduce_scatter | solution.py:316
  634.4 388.3 %reduce-scatter.24.cloned.1.call-start = ((), (), s32[]{:S(2)}) async-start(), calls=%async_computation.22 | async-start | bytes 2211840 | tf_op jit(solution)/shard_map/reduce_scatter | solution.py:313
  793.6 230.9 %reduce-scatter.32.cloned.1.call-start = ((), (), s32[]{:S(2)}) async-start(), calls=%async_computation.30 | async-start | bytes 2949120 | tf_op jit(solution)/shard_map/reduce_scatter | solution.py:325
  810.8 215.7 %reduce-scatter.30.cloned.1.call-start = ((), (), s32[]{:S(2)}) async-start(), calls=%async_computation.28 | async-start | bytes 2949120 | tf_op jit(solution)/shard_map/reduce_scatter | solution.py:322
  822.0 236.8 %reduce-scatter.28.cloned.1.call-start = ((), (), s32[]{:S(2)}) async-start(), calls=%async_computation.26 | async-start | bytes 2949120 | tf_op jit(solution)/shard_map/reduce_scatter | solution.py:319
  831.2 174.5 %copy-start.5 = (f32[512,640]{1,0:T(8,128)S(1)}, f32[512,640]{1,0:T(8,128)}, u32[]{:S(2)}) copy-start(f32[512,640]{1,0:T(8,128)} %copy-done.4) | copy-start | bytes 3932164
  831.2 174.5 %copy-start.11 = (bf16[512,640]{1,0:T(8,128)(2,1)S(1)}, bf16[512,640]{1,0:T(8,128)(2,1)}, u32[]{:S(2)}) copy-start(bf16[512,640]{1,0:T(8,128)(2,1)} %param.26) | copy-start | bytes 1966084
  831.2 174.5 %copy-start.72 = (f32[640]{0:T(1024)S(1)}, f32[640]{0:T(1024)}, u32[]{:S(2)}) copy-start(f32[640]{0:T(1024)} %copy-done.70) | copy-start | bytes 7684
  831.2 174.5 %copy-start.75 = (f32[512]{0:T(512)S(1)}, f32[512]{0:T(512)}, u32[]{:S(2)}) copy-start(f32[512]{0:T(512)} %copy-done.73) | copy-start | bytes 6148
  1005.7 18.8 %copy-start.32 = (bf16[256,640]{1,0:T(8,128)(2,1)S(1)}, bf16[256,640]{1,0:T(8,128)(2,1)}, u32[]{:S(2)}) copy-start(bf16[256,640]{1,0:T(8,128)(2,1)} %param.33) | copy-start | bytes 983044
  1008.5 18.0 %copy-start.33 = (bf16[80,2048]{1,0:T(8,128)(2,1)S(1)}, bf16[80,2048]{1,0:T(8,128)(2,1)}, u32[]{:S(2)}) copy-start(bf16[80,2048]{1,0:T(8,128)(2,1)} %param.32) | copy-start | bytes 983044
  1020.9 37.8 %copy-start.34 = (bf16[80,2048]{1,0:T(8,128)(2,1)S(1)}, bf16[80,2048]{1,0:T(8,128)(2,1)}, u32[]{:S(2)}) copy-start(bf16[80,2048]{1,0:T(8,128)(2,1)} %param.31) | copy-start | bytes 983044
  1024.5 36.1 %copy-start.31 = (f32[80,1536]{1,0:T(8,128)S(1)}, f32[80,1536]{1,0:T(8,128)}, u32[]{:S(2)}) copy-start(f32[80,1536]{1,0:T(8,128)} %get-tuple-element.121) | copy-start | bytes 1474564
  1026.5 34.9 %copy-start.35 = (f32[128,640]{1,0:T(8,128)S(1)}, f32[128,640]{1,0:T(8,128)}, u32[]{:S(2)}) copy-start(f32[128,640]{1,0:T(8,128)} %get-tuple-element.122) | copy-start | bytes 983044
  1026.5 35.7 %copy-start.23 = (f32[80,2048]{1,0:T(8,128)S(1)}, f32[80,2048]{1,0:T(8,128)}, u32[]{:S(2)}) copy-start(f32[80,2048]{1,0:T(8,128)} %get-tuple-element.123) | copy-start | bytes 1966084
  1028.5 34.5 %copy-start.21 = (f32[80,2048]{1,0:T(8,128)S(1)}, f32[80,2048]{1,0:T(8,128)}, u32[]{:S(2)}) copy-start(f32[80,2048]{1,0:T(8,128)} %get-tuple-element.124) | copy-start | bytes 1966084
  (73 other events, 302.2 us)
Sparse Core Ops, SparseCore 0:
  9.9 30.0 all-gather.11
  41.9 24.5 all-gather.13
  68.4 30.1 all-gather.15
  100.3 30.1 all-gather.17
  132.2 30.1 all-gather.19
  190.9 43.6 reduce-scatter.15
  250.3 50.2 reduce-scatter.13
  304.3 56.5 reduce-scatter.21
  364.3 56.5 reduce-scatter.19
  424.5 56.5 reduce-scatter.17
  483.9 110.8 all-reduce.3
  597.2 28.9 all-gather.23
  628.9 35.6 all-gather.21
  667.0 41.1 all-gather.29
  710.6 41.1 all-gather.27
  754.2 41.1 all-gather.25
  799.1 33.7 reduce-scatter.33
  836.4 37.3 reduce-scatter.25
  877.5 40.2 reduce-scatter.23
  921.0 43.6 reduce-scatter.31
  968.0 43.7 reduce-scatter.29
  1015.1 43.6 reduce-scatter.27
where the time goes:
time: 1080 us; the launch traced here: 1070 us
  waiting for transfers between devices  502 us (46%)
  matrix products  234 us (22%)
  blocking collectives  190 us (18%)
  other arithmetic  52.5 us (5%)
  local copies, waits for them, and re-layouts  40.8 us (4%)
  loops' own time  32.9 us (3%)
  between operations  16.5 us (2%)
    psum x1, blocking collectives, shards(): lax.psum((squares, jnp.sum(valid)), ('rep', 'fsdp'))  169 us
    psum x1, waiting for transfers between devices, shards(): lax.psum((reduced[0], reduced[1], reduced[2], reduced[3], reduced[4], red...  114 us
    reduce_scatter x1, waiting for transfers between devices, shards(): lax.psum_scatter(grad_down_part, 'fsdp', scatter_dimension=0, tiled=True)  60.4 us
    reduce_scatter x1, waiting for transfers between devices, shards(): lax.psum_scatter(grad_gate_part, 'fsdp', scatter_dimension=0, tiled=True)  60.2 us
    reduce_scatter x1, waiting for transfers between devices, shards(): lax.psum_scatter(grad_up_part, 'fsdp', scatter_dimension=0, tiled=True)  60 us
    dot_general x5, matrix products, orthogonalize(): jnp.dot(current, current.T, precision=highest, preferred_element_type=jnp...  51.3 us
    dot_general x5, matrix products, orthogonalize(): jnp.dot(mixer, current, precision=highest, preferred_element_type=jnp.flo...  48.4 us
    another operation x5, loops' own time, shards(): lax.cond(fsdp_place == owner_list[number], orthogonalize, blank, gathered...  32.9 us
  transfers between devices with their start and end apart: 26, of which 14 were waited for; matrix products, arithmetic and copies ran while one was open for 26% of the time, Pallas kernels for 0%

commit v1 on v0

--- a/solution.py
+++ b/solution.py
@@ -1,6 +1,8 @@
 import jax
 import jax.numpy as jnp
 from jax import lax
+from jax.experimental import pallas as pl
+from jax.experimental.pallas import tpu as pltpu
 from jax.sharding import PartitionSpec as P
 
 D = 640
@@ -63,27 +65,245 @@
     )
 
 
-def orthogonalize(matrix):
-    highest = lax.Precision.HIGHEST
-    row_count, col_count = matrix.shape
-    frobenius = jnp.sqrt(jnp.sum(matrix * matrix))
-    current = matrix / (frobenius + frobenius_epsilon)
-    if row_count > col_count:
-        current = current.T
-    for repeat_number in range(NS_STEPS):
-        gram = jnp.dot(current, current.T, precision=highest, preferred_element_type=jnp.float32)
-        squared = jnp.dot(gram, gram, precision=highest, preferred_element_type=jnp.float32)
-        mixer = newton_second * gram + newton_third * squared
-        current = newton_first * current + jnp.dot(
-            mixer, current, precision=highest, preferred_element_type=jnp.float32
+GROUP = 8
+MESH = pl.DeviceIdType.MESH
+f32 = jnp.float32
+bf16 = jnp.bfloat16
+
+
+def dot(a, b):
+    return lax.dot_general(a, b, (((1,), (0,)), ((), ())), preferred_element_type=f32)
+
+
+def dot_nt(a, b):
+    return lax.dot_general(a, b, (((1,), (1,)), ((), ())), preferred_element_type=f32)
+
+
+def dot_tn(a, b):
+    return lax.dot_general(a, b, (((0,), (0,)), ((), ())), preferred_element_type=f32)
+
+
+def place():
+    size = lax.axis_size("fsdp")
+    lanes = size // GROUP
+    here = lax.axis_index("fsdp")
+    return lax.axis_index("rep"), here // lanes, lax.rem(here, lanes), lanes
+
+
+OWNERS = (6, 7, 0, 2, 4)
+FLIPPED = (False, True, False, False, True)
+
+
+def gram_into(x_ref, gram):
+    rows = gram.shape[0]
+    starts = list(range(0, rows, 256))
+    for j in starts:
+        n = min(256, rows - j)
+        gram[j:rows, j : j + n] = dot_nt(x_ref[j:rows, :], x_ref[j : j + n, :])
+    for j in starts:
+        n = min(256, rows - j)
+        if j + n < rows:
+            gram[j : j + n, j + n : rows] = gram[j + n : rows, j : j + n].T
+
+
+def newton_step(x_ref, gram, mixer, high, low, first, refined):
+    gram_into(x_ref, gram)
+    rows = gram.shape[0]
+    same = lax.broadcasted_iota(jnp.int32, (rows, rows), 0) == lax.broadcasted_iota(
+        jnp.int32, (rows, rows), 1
+    )
+    whole = gram[...]
+    scale = None
+    if first:
+        scale = 1.0 / (jnp.sqrt(jnp.sum(jnp.where(same, whole, 0.0))) + frobenius_epsilon)
+        whole = whole * (scale * scale)
+        gram[...] = whole
+    high[...] = whole.astype(bf16)
+    squared = dot(high[...], high[...])
+    if refined:
+        low[...] = (gram[...] - high[...].astype(f32)).astype(bf16)
+        squared = squared + dot(high[...], low[...]) + dot(low[...], high[...])
+    mix = (
+        jnp.where(same, newton_first, 0.0) + newton_second * gram[...] + newton_third * squared
+    )
+    if first:
+        mix = mix * scale
+    mixer[...] = mix.astype(bf16)
+    width = x_ref.shape[1]
+    tile = 1024 if width % 1024 == 0 else width
+
+    @pl.loop(0, width // tile)
+    def _(t):
+        cols = pl.ds(pl.multiple_of(t * tile, tile), tile)
+        x_ref[:, cols] = dot(mixer[...], x_ref[:, cols]).astype(bf16)
+
+
+def muon_kernel(shapes, *refs):
+    grads, moments, weights = refs[0:5], refs[5:10], refs[10:15]
+    news, masters = refs[15:20], refs[20:25]
+    outgoing, arrived = refs[25:30], refs[30:35]
+    x_all, gram, mixer, high, low = refs[35:40]
+    gather_send, gather_recv, scatter_send, scatter_recv = refs[40:44]
+    rep, me, lane, lanes = place()
+
+    def device(member):
+        return (rep, member * lanes + lane)
+
+    owner_here = me == OWNERS[0]
+    for owner in OWNERS[1:]:
+        owner_here = owner_here | (me == owner)
+
+    @pl.when(owner_here)
+    def _():
+        x_all[...] = jnp.zeros_like(x_all)
+
+    barrier = pltpu.get_barrier_semaphore()
+    for step in range(1, GROUP):
+        pl.semaphore_signal(
+            barrier, inc=1, device_id=device(me ^ step), device_id_type=MESH
         )
-    if row_count > col_count:
-        current = current.T
-    return current
-
-
-def blank(matrix):
-    return jnp.zeros_like(matrix)
+
+    def block(number, member):
+        rows, cols = shapes[number]
+        if FLIPPED[number]:
+            return x_all.at[:, pl.ds(member * rows, rows)]
+        return x_all.at[pl.ds(member * rows, rows), pl.ds(0, cols)]
+
+    for number in range(5):
+        grad = grads[number][...]
+        new = momentum_decay * moments[number][...] + (1.0 - momentum_decay) * grad
+        news[number][...] = new
+        nesterov = (1.0 - momentum_decay) * grad + momentum_decay * new
+        if FLIPPED[number]:
+            nesterov = nesterov.T
+        outgoing[number][...] = nesterov.astype(bf16)
+    pl.semaphore_wait(barrier, GROUP - 1)
+
+    def gather_copy(number, member, sender):
+        rows, _ = shapes[number]
+        if FLIPPED[number]:
+            start = pl.multiple_of(sender * rows, rows)
+            target = x_all.at[:, pl.ds(start, rows)]
+        else:
+            start = pl.multiple_of(sender * rows, 16)
+            target = x_all.at[pl.ds(start, rows), pl.ds(0, shapes[number][1])]
+        return pltpu.make_async_remote_copy(
+            src_ref=outgoing[number],
+            dst_ref=target,
+            send_sem=gather_send.at[number],
+            recv_sem=gather_recv.at[sender],
+            device_id=device(member),
+            device_id_type=MESH,
+        )
+
+    for number in (2, 3, 4, 0, 1):
+
+        @pl.when(me != OWNERS[number])
+        def _():
+            gather_copy(number, OWNERS[number], me).start()
+
+    for number in range(5):
+        owner = OWNERS[number]
+
+        @pl.when(me == owner)
+        def _():
+            rows, cols = shapes[number]
+            if FLIPPED[number]:
+                x_all[:, owner * rows : (owner + 1) * rows] = outgoing[number][...]
+            else:
+                x_all[owner * rows : (owner + 1) * rows, 0:cols] = outgoing[number][...]
+            for step in range(1, GROUP):
+                gather_copy(number, owner, owner ^ step).wait_recv()
+
+    @pl.when(owner_here)
+    def _():
+        newton_step(x_all, gram, mixer, high, low, True, False)
+
+        @pl.loop(0, NS_STEPS - 3)
+        def _(k):
+            newton_step(x_all, gram, mixer, high, low, False, False)
+
+        @pl.loop(0, 2)
+        def _(k):
+            newton_step(x_all, gram, mixer, high, low, False, True)
+
+    def scatter_copy(number, member):
+        rows, cols = shapes[number]
+        return pltpu.make_async_remote_copy(
+            src_ref=block(number, member),
+            dst_ref=arrived[number],
+            send_sem=scatter_send.at[member],
+            recv_sem=scatter_recv.at[number],
+            device_id=device(member),
+            device_id_type=MESH,
+        )
+
+    for number in range(5):
+        owner = OWNERS[number]
+
+        @pl.when(me == owner)
+        def _():
+            for step in range(1, GROUP):
+                scatter_copy(number, owner ^ step).start()
+            arrived[number][...] = block(number, owner)[...]
+
+    for number in range(5):
+        owner = OWNERS[number]
+
+        @pl.when(me != owner)
+        def _():
+            scatter_copy(number, owner).wait_recv()
+
+        rows, cols = shapes[number]
+        factor = max(1.0, rows * GROUP / cols) ** 0.5 * muon_rate
+        update = arrived[number][...].astype(f32)
+        if FLIPPED[number]:
+            update = update.T
+        masters[number][...] = weights[number][...].astype(f32) - factor * update
+
+    for number in range(5):
+        owner = OWNERS[number]
+
+        @pl.when(me == owner)
+        def _():
+            for step in range(1, GROUP):
+                scatter_copy(number, owner ^ step).wait_send()
+
+        @pl.when(me != owner)
+        def _():
+            gather_copy(number, owner, me).wait_send()
+
+
+def muon(grads, moments, weights):
+    shapes = tuple(g.shape for g in grads)
+    flipped = [s[::-1] if flip else s for s, flip in zip(shapes, FLIPPED)]
+    side = flipped[0][0] * GROUP
+    width = max(s[1] if not flip else s[1] * GROUP for s, flip in zip(flipped, FLIPPED))
+    vmem = pl.BlockSpec(memory_space=pltpu.VMEM)
+    out = pl.pallas_call(
+        lambda *refs: muon_kernel(shapes, *refs),
+        out_shape=[jax.ShapeDtypeStruct(s, f32) for s in shapes + shapes],
+        in_specs=[vmem] * 15,
+        out_specs=[vmem] * 10,
+        scratch_shapes=[pltpu.VMEM(s, bf16) for s in flipped]
+        + [pltpu.VMEM(s, bf16) for s in flipped]
+        + [
+            pltpu.VMEM((side, width), bf16),
+            pltpu.VMEM((side, side), f32),
+            pltpu.VMEM((side, side), bf16),
+            pltpu.VMEM((side, side), bf16),
+            pltpu.VMEM((side, side), bf16),
+            pltpu.SemaphoreType.DMA((5,)),
+            pltpu.SemaphoreType.DMA((GROUP,)),
+            pltpu.SemaphoreType.DMA((GROUP,)),
+            pltpu.SemaphoreType.DMA((5,)),
+        ],
+        compiler_params=pltpu.CompilerParams(
+            collective_id=1, has_side_effects=True, vmem_limit_bytes=60 * 2**20
+        ),
+        name="muon",
+    )(*grads, *moments, *weights)
+    return out[:5], out[5:]
 
 
 def shards(
@@ -108,7 +328,6 @@
     fsdp_size = lax.axis_size("fsdp")
     fsdp_place = lax.axis_index("fsdp")
     rep_place = lax.axis_index("rep")
-    owner_list = [number * fsdp_size // 5 for number in range(5)]
     parity = fsdp_place % 2
     sequence_id = (rep_place * fsdp_size + fsdp_place) // 2
     table_ids = jnp.arange(prefix.shape[0], dtype=jnp.int32)
@@ -188,15 +407,8 @@
     )
     total_squares, total_count = lax.psum((squares, jnp.sum(valid)), ("rep", "fsdp"))
     statistics = jnp.sqrt(total_squares / (total_count * D))
-    qkv_back, out_back = (
-        lax.all_gather(w_qkv, "fsdp", axis=0, tiled=True),
-        lax.all_gather(w_out, "fsdp", axis=0, tiled=True),
-    )
-    gate_back, up_back, down_back = (
-        lax.all_gather(w_gate, "fsdp", axis=0, tiled=True),
-        lax.all_gather(w_up, "fsdp", axis=0, tiled=True),
-        lax.all_gather(w_down, "fsdp", axis=0, tiled=True),
-    )
+    qkv_back, out_back = qkv_whole, out_whole
+    gate_back, up_back, down_back = gate_whole, up_whole, down_whole
     upstream = cotangent.astype(jnp.float32)
     d_branch_two, d_gain_three = second_back(upstream)
     d_branch_two_low = d_branch_two.astype(jnp.bfloat16)
@@ -271,70 +483,44 @@
     grad_tokens = d_hidden + d_residual_norm
     grad_gains_part = jnp.stack([d_gain_zero, d_gain_one, d_gain_two, d_gain_three], axis=1)
     reduced = (
-        lax.psum_scatter(grad_qkv_part, "fsdp", scatter_dimension=0, tiled=True),
-        lax.psum_scatter(grad_out_part, "fsdp", scatter_dimension=0, tiled=True),
-        lax.psum_scatter(grad_gate_part, "fsdp", scatter_dimension=0, tiled=True),
-        lax.psum_scatter(grad_up_part, "fsdp", scatter_dimension=0, tiled=True),
-        lax.psum_scatter(grad_down_part, "fsdp", scatter_dimension=0, tiled=True),
+        lax.psum_scatter(grad_qkv_part.astype(jnp.bfloat16), "fsdp", scatter_dimension=0, tiled=True),
+        lax.psum_scatter(grad_out_part.astype(jnp.bfloat16), "fsdp", scatter_dimension=0, tiled=True),
+        lax.psum_scatter(grad_gate_part.astype(jnp.bfloat16), "fsdp", scatter_dimension=0, tiled=True),
+        lax.psum_scatter(grad_up_part.astype(jnp.bfloat16), "fsdp", scatter_dimension=0, tiled=True),
+        lax.psum_scatter(grad_down_part.astype(jnp.bfloat16), "fsdp", scatter_dimension=0, tiled=True),
         lax.psum_scatter(grad_gains_part, "fsdp", scatter_dimension=0, tiled=True),
     )
     reduced = lax.psum(
-        (reduced[0], reduced[1], reduced[2], reduced[3], reduced[4], reduced[5]), "rep"
+        tuple(term.astype(jnp.float32) for term in reduced), "rep"
     )
     moments = (moment_qkv, moment_out, moment_gate, moment_up, moment_down)
     weight_shards = (w_qkv, w_out, w_gate, w_up, w_down)
-    full_shapes = [(shard.shape[0] * fsdp_size, shard.shape[1]) for shard in weight_shards]
-    new_moments = tuple(
-        (
-            momentum_decay * moments[number] + (1.0 - momentum_decay) * reduced[number]
-            for number in range(5)
-        )
-    )
-    nesterov = tuple(
-        (
-            (1.0 - momentum_decay) * reduced[number] + momentum_decay * new_moments[number]
-            for number in range(5)
-        )
-    )
-    gathered = (
-        lax.all_gather(nesterov[0], "fsdp", axis=0, tiled=True),
-        lax.all_gather(nesterov[1], "fsdp", axis=0, tiled=True),
-        lax.all_gather(nesterov[2], "fsdp", axis=0, tiled=True),
-        lax.all_gather(nesterov[3], "fsdp", axis=0, tiled=True),
-        lax.all_gather(nesterov[4], "fsdp", axis=0, tiled=True),
-    )
-    results = tuple(
-        (
-            lax.cond(fsdp_place == owner_list[number], orthogonalize, blank, gathered[number])
-            for number in range(5)
-        )
-    )
-    ortho_shards = (
-        lax.psum_scatter(
-            results[0].astype(jnp.bfloat16), "fsdp", scatter_dimension=0, tiled=True
-        ).astype(jnp.float32),
-        lax.psum_scatter(
-            results[1].astype(jnp.bfloat16), "fsdp", scatter_dimension=0, tiled=True
-        ).astype(jnp.float32),
-        lax.psum_scatter(
-            results[2].astype(jnp.bfloat16), "fsdp", scatter_dimension=0, tiled=True
-        ).astype(jnp.float32),
-        lax.psum_scatter(
-            results[3].astype(jnp.bfloat16), "fsdp", scatter_dimension=0, tiled=True
-        ).astype(jnp.float32),
-        lax.psum_scatter(
-            results[4].astype(jnp.bfloat16), "fsdp", scatter_dimension=0, tiled=True
-        ).astype(jnp.float32),
-    )
-    masters = tuple(
-        (
-            weight_shards[number].astype(jnp.float32)
-            - muon_rate
-            * max(1.0, full_shapes[number][0] / full_shapes[number][1]) ** 0.5
-            * ortho_shards[number]
-            for number in range(5)
-        )
-    )
+    lanes = fsdp_size // GROUP
+    if lanes > 1:
+        teams = [[member * lanes + lane for lane in range(lanes)] for member in range(GROUP)]
+
+        def joined(shard):
+            return lax.all_gather(shard, "fsdp", axis=0, tiled=True, axis_index_groups=teams)
+
+        def parted(block):
+            size = block.shape[0] // lanes
+            start = lax.rem(fsdp_place, lanes) * size
+            return lax.dynamic_slice_in_dim(block, start, size, 0)
+    else:
+
+        def joined(shard):
+            return shard
+
+        def parted(block):
+            return block
+
+    new_moments, masters = muon(
+        [joined(term) for term in reduced[:5]],
+        [joined(term) for term in moments],
+        [joined(term) for term in weight_shards],
+    )
+    new_moments = [parted(term) for term in new_moments]
+    masters = [parted(term) for term in masters]
     gain_grad = reduced[5]
     gains_local = gains.astype(jnp.float32)
     first_new = first_decay * gain_first + (1.0 - first_decay) * gain_grad

time: 1080 us -> 705 us (0.65)
  waiting for transfers between devices: 502 us -> 284 us
  matrix products: 234 us -> 109 us
  Pallas kernels: 0 us -> 71.1 us
  blocking collectives: 190 us -> 152 us
  loops' own time: 32.9 us -> 0 us
  other arithmetic: 52.5 us -> 30.8 us
    psum x1, blocking collectives: 169 us -> 39.7 us  [shards(): lax.psum((squares, jnp.sum(valid)), ('rep', 'fsdp'))]
    dot_general x15 -> x0, matrix products: 123 us -> none  [the longest x5 51.3 us: orthogonalize(): jnp.dot(current, current.T, precision=highest, preferred_element_type=jnp...]
    psum x1 -> x0, waiting for transfers between devices: 114 us -> none  [shards(): lax.psum((reduced[0], reduced[1], reduced[2], reduced[3], reduced[4], red...]
    psum x1, blocking collectives: 10.9 us -> 102 us  [shards(): lax.psum(tuple((term.astype(jnp.float32) for term in reduced)), 'rep')]
    pallas_call x0 -> x1, Pallas kernels: none -> 71.1 us  [muon(): pl.pallas_call(lambda *refs: muon_kernel(shapes, *refs), out_shape=[jax.S...]
    reduce_scatter x10 -> x5, waiting for transfers between devices: 242 us -> 190 us  [the longest x1 47.4 us: shards(): lax.psum_scatter(grad_down_part.astype(jnp.bfloat16), 'fsdp', scatter_dim...]
    all_gather x5 -> x0, waiting for transfers between devices: 46.1 us -> none  [the longest x1 30 us: shards(): lax.all_gather(nesterov[0], 'fsdp', axis=0, tiled=True)]
    another operation x5 -> x0, loops' own time: 32.9 us -> none  [shards(): lax.cond(fsdp_place == owner_list[number], orthogonalize, blank, gathered...]
  transfers between devices with their start and end apart: 26 -> 15, of which waited for: 14 -> 11; matrix products, arithmetic and copies ran while one was open for 26% -> 17% of each run, Pallas kernels for 0% -> 0%
where the time goes in v1:
time: 705 us; the launch traced here: 698 us
  waiting for transfers between devices  284 us (40%)
  blocking collectives  152 us (22%)
  matrix products  109 us (15%)
  Pallas kernels  71.1 us (10%)
  local copies, waits for them, and re-layouts  33.2 us (5%)
  other arithmetic  30.8 us (4%)
  between operations  15.6 us (2%)
    psum x1, blocking collectives, shards(): lax.psum(tuple((term.astype(jnp.float32) for term in reduced)), 'rep')  102 us
    pallas_call x1, Pallas kernels, muon(): pl.pallas_call(lambda *refs: muon_kernel(shapes, *refs), out_shape=[jax.S...  71.1 us
    reduce_scatter x1, waiting for transfers between devices, shards(): lax.psum_scatter(grad_down_part.astype(jnp.bfloat16), 'fsdp', scatter_dim...  47.4 us
    reduce_scatter x1, waiting for transfers between devices, shards(): lax.psum_scatter(grad_gate_part.astype(jnp.bfloat16), 'fsdp', scatter_dim...  47.4 us
    reduce_scatter x1, waiting for transfers between devices, shards(): lax.psum_scatter(grad_up_part.astype(jnp.bfloat16), 'fsdp', scatter_dimen...  47.2 us
    reduce_scatter x1, waiting for transfers between devices, shards(): lax.psum_scatter(grad_qkv_part.astype(jnp.bfloat16), 'fsdp', scatter_dime...  43.7 us
    psum x1, blocking collectives, shards(): lax.psum((squares, jnp.sum(valid)), ('rep', 'fsdp'))  39.7 us
    all_gather x1, waiting for transfers between devices, shards(): lax.all_gather(w_up, 'fsdp', axis=0, tiled=True)  26.2 us
  transfers between devices with their start and end apart: 15, of which 11 were waited for; matrix products, arithmetic and copies ran while one was open for 17% of the time, Pallas kernels for 0%

profile of v1, /device:TPU:0, one launch (start us, length us, event | category | flops | bytes accessed | tf_op | source)
XLA Modules:
  0.0 698.2 jit_solution(13636002337006040823)
XLA Ops:
  11.2 1.3 fusion.80
  13.2 1.3 fusion.43
  14.5 10.4 %all-gather = bf16[8,80,4]{1,2,0:T(4,128)(2,1)S(1)} all-gather(bf16[1,80,4]{1,2,0:T(4,128)(2,1)S(1)} %bitcast.116), channel_id=1, replica_groups=mesh['rep'=4,'fsdp'=8] {'fsdp'}, dimensions={0}, use_global_device_ids=true | all-gather | bytes 5760 | tf_op jit(solution)/shard_map/all_gather | solution.py:342
  26.2 13.8 %all-gather.7.cloned.1.call-done = bf16[640,1536]{1,0:T(8,128)(2,1)} async-done(((bf16[80,1536]{1,0:T(8,128)(2,1)}), bf16[640,1536]{1,0:T(8,128)(2,1)}) %all-gather.7.cloned.1.call-update) | async-done | bytes 1966096 | tf_op jit(solution)/shard_map/all_gather | solution.py:340
  40.0 3.0 fusion.70
  43.3 1.4 copy-done.5
  44.9 2.0 reshape.266
  46.9 1.7 fusion.100
  48.7 2.8 fusion.55
  53.1 1.3 fusion.45
  54.5 5.6 fusion.101
  60.1 3.2 copy-done.72
  63.3 2.3 fusion.29
  66.5 2.7 multiply_reduce_fusion.9
  72.5 26.1 %all-gather.11.cloned.1.call-done = bf16[640,2048]{1,0:T(8,128)(2,1)} async-done(((bf16[80,2048]{1,0:T(8,128)(2,1)}), bf16[640,2048]{1,0:T(8,128)(2,1)}) %all-gather.11.cloned.1.call-update) | async-done | bytes 2621456 | tf_op jit(solution)/shard_map/all_gather | solution.py:345
  98.6 5.7 fusion.102
  104.3 26.2 %all-gather.13.cloned.1.call-done = bf16[640,2048]{1,0:T(8,128)(2,1)} async-done(((bf16[80,2048]{1,0:T(8,128)(2,1)}), bf16[640,2048]{1,0:T(8,128)(2,1)}) %all-gather.13.cloned.1.call-update) | async-done | bytes 2621456 | tf_op jit(solution)/shard_map/all_gather | solution.py:346
  130.5 8.2 %multiply_convert_fusion.1 = (bf16[512,2048]{1,0:T(8,128)(2,1)}, f32[512,2048]{1,0:T(8,128)}) fusion(f32[512,2048]{1,0:T(8,128)} %fusion.102, bf16[512,640]{1,0:T(8,128)(2,1)} %multiply_convert_fusion.2, bf16[640,2048]{1,0:T(8,128)(2,1)} %all-gather.13.cloned.1.call-done), kind=kOutput, calls=%fused_computation.23 | convolution fusion | flops 1352663040 | bytes 13762560 | tf_op jit(solution)/shard_map/dot_general | solution.py:395
  138.7 23.7 %all-gather.15.cloned.1.call-done = bf16[2048,640]{1,0:T(8,128)(2,1)} async-done(((bf16[256,640]{1,0:T(8,128)(2,1)}), bf16[2048,640]{1,0:T(8,128)(2,1)}) %all-gather.15.cloned.1.call-update) | async-done | bytes 2621456 | tf_op jit(solution)/shard_map/all_gather | solution.py:347
  162.3 4.4 multiply_reduce_fusion.7
  168.6 2.2 multiply_reduce_fusion
  170.9 6.0 multiply_convert_fusion
  177.0 1.8 fusion.103
  180.2 2.0 multiply_reduce_fusion.3
  182.8 1.5 multiply_reduce_fusion.4
  187.9 4.7 fusion.33
  193.7 4.5 fusion.52
  198.3 18.7 %fusion.32 = f32[1024,256]{1,0:T(8,128)} fusion(f32[1024,512,4]{1,0,2:T(8,128)} %fusion.52, f32[1024,512,4]{1,0,2:T(8,128)} %copy-done, bf16[512,4,128]{2,0,1:T(8,128)(2,1)S(1)} %copy-done.9, bf16[512,4,128]{2,0,1:T(8,128)(2,1)S(1)} %copy-done.7, f32[4,512,1024]{1,2,0:T(8,128)} %copy-done.72, f32[4,512]{1,0:T(4,128)S(1)} %copy-done.74), kind=kOutput, calls=%fused_computation.64 | convolution fusion | flops 1098910720 | bytes 27271168 | tf_op jit(solution)/shard_map/hrk,rhd->kd/dot_general | solution.py:451
  217.0 1.8 dynamic-slice_convert_fusion.1
  219.0 18.1 %fusion.24 = f32[512,4,256]{2,0,1:T(8,128)S(1)} fusion(f32[1024,512,4]{1,0,2:T(8,128)} %fusion.52, f32[1024,512,4]{1,0,2:T(8,128)} %copy-done, bf16[512,256]{1,0:T(8,128)(2,1)} %copy-done.34, bf16[512,128]{1,0:T(8,128)(2,1)S(1)} %copy-done.11, bf16[512,128]{1,0:T(8,128)(2,1)S(1)} %copy-done.13, pred[]{:T(512)S(6)} %eq.11, f32[4,512,1024]{1,2,0:T(8,128)} %copy-done.72, ...), kind=kOutput, calls=%fused_computation.55 | convolution fusion | flops 1100221440 | bytes 27795456 | tf_op jit(solution)/shard_map/hrk,kd->rhd/dot_general | solution.py:450
  242.0 3.8 fusion.37
  246.8 3.4 convolution_convert_fusion.4
  250.3 2.8 convolution_convert_fusion.3
  253.2 4.9 convolution_convert_fusion.2
  259.2 4.7 convolution_convert_fusion.1
  265.0 4.9 convolution_convert_fusion
  271.8 2.7 pad_maximum_fusion.9
  274.5 39.7 %all-reduce = (f32[4]{0:T(128)S(1)}, f32[]{:T(128)}) all-reduce(f32[4]{0:T(128)S(1)} %pad_maximum_fusion.9, f32[]{:T(128)} %get-tuple-element.56), channel_id=1, replica_groups=mesh['rep'=4,'fsdp'=8] {'rep','fsdp'}, use_global_device_ids=true, to_apply=%region_35.36 | all-reduce | flops 5 | bytes 40 | tf_op jit(solution)/shard_map/psum | solution.py:408
  315.4 1.4 fusion.42
  317.6 3.9 reduce-scatter.11.cloned.1.call-done
  321.5 43.7 %reduce-scatter.9.cloned.1.call-done = bf16[80,1536]{1,0:T(8,128)(2,1)} async-done(((bf16[640,1536]{1,0:T(8,128)(2,1)}), bf16[80,1536]{1,0:T(8,128)(2,1)}) %reduce-scatter.9.cloned.1.call-update) | async-done | bytes 245776 | tf_op jit(solution)/shard_map/reduce_scatter | solution.py:486
  365.3 47.4 %reduce-scatter.13.cloned.1.call-done = bf16[80,2048]{1,0:T(8,128)(2,1)} async-done(((bf16[640,2048]{1,0:T(8,128)(2,1)}), bf16[80,2048]{1,0:T(8,128)(2,1)}) %reduce-scatter.13.cloned.1.call-update) | async-done | bytes 327696 | tf_op jit(solution)/shard_map/reduce_scatter | solution.py:488
  412.6 47.2 %reduce-scatter.15.cloned.1.call-done = bf16[80,2048]{1,0:T(8,128)(2,1)} async-done(((bf16[640,2048]{1,0:T(8,128)(2,1)}), bf16[80,2048]{1,0:T(8,128)(2,1)}) %reduce-scatter.15.cloned.1.call-update) | async-done | bytes 327696 | tf_op jit(solution)/shard_map/reduce_scatter | solution.py:489
  459.8 47.4 %reduce-scatter.17.cloned.1.call-done = bf16[256,640]{1,0:T(8,128)(2,1)} async-done(((bf16[2048,640]{1,0:T(8,128)(2,1)}), bf16[256,640]{1,0:T(8,128)(2,1)}) %reduce-scatter.17.cloned.1.call-update) | async-done | bytes 327696 | tf_op jit(solution)/shard_map/reduce_scatter | solution.py:490
  507.2 102.3 %all-reduce.3 = (f32[80,1536]{1,0:T(8,128)}, f32[128,640]{1,0:T(8,128)}, f32[80,2048]{1,0:T(8,128)}, f32[80,2048]{1,0:T(8,128)}, f32[256,640]{1,0:T(8,128)}, /*index=5*/f32[80,4]{0,1:T(4,128)S(1)}) all-reduce(bf16[80,1536]{1,0:T(8,128)(2,1)} %reduce-scatter.9.cloned.1.call-done, ...), channel_id=1, replica_groups=mesh['rep'=4,'fsdp'=8] {'rep'}, use_global_device_ids=true, to_apply=%region_13.14 | all-reduce | flops 696640 | bytes 4180480 | tf_op jit(solution)/shard_map/psum | solution.py:493
  609.6 71.1 %muon.1 = (f32[80,1536]{1,0:T(8,128)}, f32[128,640]{1,0:T(8,128)}, f32[80,2048]{1,0:T(8,128)}, f32[80,2048]{1,0:T(8,128)}, f32[256,640]{1,0:T(8,128)}, /*index=5...) custom-call(f32[80,1536]{1,0:T(8,128)} %get-tuple-element.130.refs_0_, ...), custom_call_target="tpu_custom_call" | custom-call | tf_op jit(solution)/shard_map/muon/pallas_call | solution.py:283
  681.3 1.9 copy.151
  683.2 1.7 copy.152
  (232 shorter events, 39.2 us)
Async XLA Ops:
  7.2 32.8 %copy-start.4 = (bf16[512,640]{1,0:T(8,128)(2,1)S(1)}, bf16[512,640]{1,0:T(8,128)(2,1)}, u32[]{:S(2)}) copy-start(bf16[512,640]{1,0:T(8,128)(2,1)} %param.16) | copy-start | bytes 1966084
  7.2 7.3 %copy-start.56 = (bf16[80,4]{0,1:T(4,128)(2,1)S(1)}, bf16[80,4]{0,1:T(4,128)(2,1)}, u32[]{:S(2)}) copy-start(bf16[80,4]{0,1:T(4,128)(2,1)} %param.24) | copy-start | bytes 1924
  7.2 32.8 %all-gather.7.cloned.1.call-start = ((), (), s32[]{:S(2)}) async-start(), calls=%async_computation.6 | async-start | bytes 2211840 | tf_op jit(solution)/shard_map/all_gather | solution.py:340
  7.9 58.6 %all-gather.9.cloned.1.call-start = ((), (), s32[]{:S(2)}) async-start(), calls=%async_computation.7 | async-start | bytes 1474560 | tf_op jit(solution)/shard_map/all_gather | solution.py:341
  8.7 89.9 %all-gather.11.cloned.1.call-start = ((), (), s32[]{:S(2)}) async-start(), calls=%async_computation.8 | async-start | bytes 2949120 | tf_op jit(solution)/shard_map/all_gather | solution.py:345
  9.4 121.0 %all-gather.13.cloned.1.call-start = ((), (), s32[]{:S(2)}) async-start(), calls=%async_computation.9 | async-start | bytes 2949120 | tf_op jit(solution)/shard_map/all_gather | solution.py:346
  10.0 152.3 %all-gather.15.cloned.1.call-start = ((), (), s32[]{:S(2)}) async-start(), calls=%async_computation.10 | async-start | bytes 2949120 | tf_op jit(solution)/shard_map/all_gather | solution.py:347
  10.6 306.2 %reduce-scatter.19.cloned.1.call-start = ((), (), s32[]{:S(2)}) async-start(), calls=%async_computation.16 | async-start | bytes 368640
  11.2 37.4 %copy-start.35 = (f32[512]{0:T(512)}, f32[512]{0:T(512)S(1)}, u32[]{:S(2)}) copy-start(f32[512]{0:T(512)S(1)} %fusion.76) | copy-start | bytes 6148
  14.5 10.4 %copy-start.41 = (f32[512]{0:T(512)}, f32[512]{0:T(512)S(1)}, u32[]{:S(2)}) copy-start(f32[512]{0:T(512)S(1)} %fusion.43) | copy-start | bytes 6148
  14.5 28.5 %copy-start.48 = (f32[512]{0:T(512)}, f32[512]{0:T(512)S(1)}, u32[]{:S(2)}) copy-start(f32[512]{0:T(512)S(1)} %fusion.74) | copy-start | bytes 6148
  25.0 18.0 %copy-start.43 = (f32[640]{0:T(1024)}, f32[640]{0:T(1024)S(1)}, u32[]{:S(2)}) copy-start(f32[640]{0:T(1024)S(1)} %get-tuple-element.55) | copy-start | bytes 7684
  43.1 17.0 %copy-start.14 = (bf16[512,256]{1,0:T(8,128)(2,1)}, bf16[512,256]{1,0:T(8,128)(2,1)S(1)}, u32[]{:S(2)}) copy-start(bf16[512,256]{1,0:T(8,128)(2,1)S(1)} %slice.91) | copy-start | bytes 786436
  44.7 15.4 %collective-permute-start = (bf16[512,256]{1,0:T(8,128)(2,1)S(1)}, bf16[512,256]{1,0:T(8,128)(2,1)S(1)}, u32[]{:S(2)}, u32[]{:S(2)}) collective-permute-start(bf16[512,256]{1,0:T(8,128)(2,1)S(1)} %slice.91), channel_id=1, source_target_pairs={{0,1},{1,0},{2,3},{3,2},{4,5},{5,4},{6,7},{7,6},{8,9},{9,8},{10,11... | collective-permute-start | bytes 786440 | tf_op jit(solution)/shard_map/ppermute | solution.py:33
  51.5 1.6 collective-permute-start.1
  54.5 5.6 copy-start
  60.1 5.6 copy-start.73
  60.1 5.5 copy-start.32
  162.3 4.4 copy-start.3
  162.3 8.5 %copy-start.71 = (f32[512,2048]{1,0:T(8,128)S(1)}, f32[512,2048]{1,0:T(8,128)}, u32[]{:S(2)}) copy-start(f32[512,2048]{1,0:T(8,128)} %get-tuple-element.101) | copy-start | bytes 12582916
  166.8 4.1 copy-start.68
  170.8 6.0 copy-start.17
  170.9 6.1 copy-start.64
  187.9 5.9 copy-start.15
  187.9 5.8 copy-start.33
  193.5 4.8 copy-start.7
  193.5 4.8 copy-start.9
  193.5 47.4 %collective-permute-start.3 = (bf16[512,256]{0,1:T(8,128)(2,1)}, bf16[512,256]{0,1:T(8,128)(2,1)}, u32[]{:S(2)}, u32[]{:S(2)}) collective-permute-start(bf16[512,256]{0,1:T(8,128)(2,1)} %dynamic-slice_convert_fusion), channel_id=1, source_target_pairs={{0,1},{1,0},{2,3},{3,2},{4,5},{5,4},{6,7},{7,6},{8,9},{9,8},{10,11... | collective-permute-start | bytes 786440 | tf_op jit(solution)/shard_map/ppermute | solution.py:33
  198.2 20.8 %copy-start.11 = (bf16[512,128]{1,0:T(8,128)(2,1)S(1)}, bf16[512,128]{1,0:T(8,128)(2,1)}, u32[]{:S(2)}) copy-start(bf16[512,128]{1,0:T(8,128)(2,1)} %copy-done.10) | copy-start | bytes 393220
  198.3 20.8 %copy-start.13 = (bf16[512,128]{1,0:T(8,128)(2,1)S(1)}, bf16[512,128]{1,0:T(8,128)(2,1)}, u32[]{:S(2)}) copy-start(bf16[512,128]{1,0:T(8,128)(2,1)} %copy-done.12) | copy-start | bytes 393220
  218.8 18.4 %copy-start.16 = (f32[512,128]{1,0:T(8,128)S(1)}, f32[512,128]{1,0:T(8,128)}, u32[]{:S(2)}) copy-start(f32[512,128]{1,0:T(8,128)} %get-tuple-element.90) | copy-start | bytes 786436
  218.8 19.4 %collective-permute-start.2 = (bf16[512,256]{1,0:T(8,128)(2,1)}, bf16[512,256]{1,0:T(8,128)(2,1)}, u32[]{:S(2)}, u32[]{:S(2)}) collective-permute-start(bf16[512,256]{1,0:T(8,128)(2,1)} %dynamic-slice_convert_fusion.1), channel_id=1, source_target_pairs={{0,1},{1,0},{2,3},{3,2},{4,5},{5,4},{6,7},{7,6},{8,9},{9,8},{10,11... | collective-permute-start | bytes 786440 | tf_op jit(solution)/shard_map/ppermute | solution.py:33
  238.1 3.8 copy-start.44
  242.0 3.8 copy-start.45
  242.0 3.8 copy-start.46
  246.8 74.7 %reduce-scatter.11.cloned.1.call-start = ((), (), s32[]{:S(2)}) async-start(), calls=%async_computation.12 | async-start | bytes 1474560 | tf_op jit(solution)/shard_map/reduce_scatter | solution.py:487
  250.3 115.0 %reduce-scatter.9.cloned.1.call-start = ((), (), s32[]{:S(2)}) async-start(), calls=%async_computation.11 | async-start | bytes 2211840 | tf_op jit(solution)/shard_map/reduce_scatter | solution.py:486
  253.1 159.5 %reduce-scatter.13.cloned.1.call-start = ((), (), s32[]{:S(2)}) async-start(), calls=%async_computation.13 | async-start | bytes 2949120 | tf_op jit(solution)/shard_map/reduce_scatter | solution.py:488
  258.1 201.7 %reduce-scatter.15.cloned.1.call-start = ((), (), s32[]{:S(2)}) async-start(), calls=%async_computation.14 | async-start | bytes 2949120 | tf_op jit(solution)/shard_map/reduce_scatter | solution.py:489
  263.9 243.3 %reduce-scatter.17.cloned.1.call-start = ((), (), s32[]{:S(2)}) async-start(), calls=%async_computation.15 | async-start | bytes 2949120 | tf_op jit(solution)/shard_map/reduce_scatter | solution.py:490
  269.9 45.5 %copy-start.2 = (f32[512,640]{1,0:T(8,128)S(1)}, f32[512,640]{1,0:T(8,128)}, u32[]{:S(2)}) copy-start(f32[512,640]{1,0:T(8,128)} %copy-done.1) | copy-start | bytes 3932164
  609.5 71.1 %copy-start.60 = (f32[80,4]{0,1:T(4,128)}, f32[80,4]{0,1:T(4,128)S(1)}, u32[]{:S(2)}) copy-start(f32[80,4]{0,1:T(4,128)S(1)} %get-tuple-element.135) | copy-start | bytes 3844
  609.5 71.2 %copy-start.57 = (bf16[80,4]{0,1:T(4,128)(2,1)S(1)}, bf16[80,4]{0,1:T(4,128)(2,1)}, u32[]{:S(2)}) copy-start(bf16[80,4]{0,1:T(4,128)(2,1)} %param.24) | copy-start | bytes 1924
  609.5 71.2 %copy-start.58 = (f32[80,4]{0,1:T(4,128)S(1)}, f32[80,4]{0,1:T(4,128)}, u32[]{:S(2)}) copy-start(f32[80,4]{0,1:T(4,128)} %param.31) | copy-start | bytes 3844
  609.6 71.2 %copy-start.59 = (f32[80,4]{0,1:T(4,128)S(1)}, f32[80,4]{0,1:T(4,128)}, u32[]{:S(2)}) copy-start(f32[80,4]{0,1:T(4,128)} %param.30) | copy-start | bytes 3844
  680.7 4.3 copy-start.25
  680.7 5.1 copy-start.24
  681.3 5.3 copy-start.23
  (42 other events, 77.2 us)
Sparse Core Ops, SparseCore 0:
  9.9 30.0 all-gather.6
  41.9 24.5 all-gather.8
  68.4 30.1 all-gather.10
  100.3 30.1 all-gather.12
  132.2 30.1 all-gather.14
  246.9 33.7 reduce-scatter.18
  283.9 37.5 reduce-scatter.10
  324.9 40.2 reduce-scatter.8
  368.9 43.6 reduce-scatter.12
  416.2 43.6 reduce-scatter.14
  463.5 43.6 reduce-scatter.16

commit v2 on v1

v2 whole, which is shorter than its diff:
```python
import jax
import jax.numpy as jnp
from jax import lax
from jax.experimental import pallas as pl
from jax.experimental.pallas import tpu as pltpu
from jax.sharding import PartitionSpec as P

HEADS = 4
HEAD_DIM = 256
NS_STEPS = 5
ADAM_STEP = 10


norm_epsilon = 1e-06
soft_cap = 50.0
rotary_base = 10000.0
newton_first = 3.4445
newton_second = -4.775
newton_third = 2.0315
momentum_decay = 0.95
muon_rate = 1.0
first_decay = 0.9
second_decay = 0.95
adam_rate = 1.0
weight_decay = 0.1
adam_epsilon = 1e-08
frobenius_epsilon = 1e-07

GROUP = 8
MESH = pl.DeviceIdType.MESH
f32 = jnp.float32
bf16 = jnp.bfloat16


def dot(a, b):
    return lax.dot_general(a, b, (((1,), (0,)), ((), ())), preferred_element_type=f32)


def dot_nt(a, b):
    return lax.dot_general(a, b, (((1,), (1,)), ((), ())), preferred_element_type=f32)


def dot_tn(a, b):
    return lax.dot_general(a, b, (((0,), (0,)), ((), ())), preferred_element_type=f32)


def place():
    size = lax.axis_size("fsdp")
    lanes = size // GROUP
    here = lax.axis_index("fsdp")
    return lax.axis_index("rep"), here // lanes, lax.rem(here, lanes), lanes


def rotary_tables(positions, head_dim):
    half_dim = head_dim // 2
    frequency = rotary_base ** (-(jnp.arange(half_dim, dtype=f32) * 2.0 / head_dim))
    angles = positions.astype(f32)[:, None] * frequency[None, :]
    return (jnp.cos(angles), jnp.sin(angles))


QKV, OUT, GATE, UP, DOWN = range(5)
CORE, ACROSS, ALONG = 1, 2, 4
PAIRS = (
    ((GATE, 0), (UP, 0)),
    ((DOWN, 0), (GATE, 1)),
    ((UP, 1), (DOWN, 1)),
    ((OUT, 0), (OUT, 1)),
    ((QKV, 0), (QKV, 1)),
)
CHUNK = 128
TILE = 256


def split_shape(number, shape):
    rows, cols = shape
    return (rows // 2, cols) if number in (OUT, DOWN) else (rows, cols // 2)


def layer_names(rows, keys, width, shapes, reps):
    halves = [split_shape(number, shape) for number, shape in enumerate(shapes)]
    feats = HEADS * HEAD_DIM
    inner = shapes[GATE][1]
    spaces = {}
    for number, (height, cols) in enumerate(shapes):
        spaces[f"whole{number}"] = pltpu.VMEM((height * GROUP, cols), bf16)
    spaces.update(
        gain_parts=pltpu.VMEM((GROUP, 8, width), f32),
        gains=pltpu.VMEM((8, width), f32),
        normed=pltpu.VMEM((rows, width), bf16),
        one_t=pltpu.VMEM((width, rows), bf16),
        two_t=pltpu.VMEM((width, rows), bf16),
        proj=pltpu.VMEM((rows, feats + 2 * HEAD_DIM), bf16),
        key=pltpu.VMEM((keys, HEAD_DIM), bf16),
        value=pltpu.VMEM((keys, HEAD_DIM), bf16),
        key_t=pltpu.VMEM((HEAD_DIM, keys), bf16),
        value_t=pltpu.VMEM((HEAD_DIM, keys), bf16),
        att=pltpu.VMEM((rows, feats), bf16),
        att_t=pltpu.VMEM((feats, rows), bf16),
        inverse=pltpu.VMEM((8, rows), f32),
        branch=pltpu.VMEM((rows, width), f32),
        hidden=pltpu.VMEM((rows, width), f32),
        slope=pltpu.VMEM((rows, inner), bf16),
        bend=pltpu.VMEM((rows, inner), bf16),
        active=pltpu.VMEM((rows, inner), bf16),
        d_key=pltpu.VMEM((keys, HEAD_DIM), f32),
        d_value=pltpu.VMEM((keys, HEAD_DIM), f32),
        swap_out=pltpu.VMEM((2, rows, HEAD_DIM), bf16),
        swap_in=pltpu.VMEM((2, rows, HEAD_DIM), bf16),
        squares=pltpu.VMEM((8, width), f32),
        d_gains=pltpu.VMEM((8, width), f32),
        small_parts=pltpu.VMEM((GROUP, 8, width), f32),
        small_reps=pltpu.VMEM((reps, 8, width), f32),
    )
    for number, half in enumerate(halves):
        spaces[f"stage{number}"] = pltpu.VMEM((2, 2, 2, 2) + half, bf16)
        spaces[f"chip{number}"] = pltpu.VMEM((2, 2, 2) + half, bf16)
        spaces[f"pair{number}"] = pltpu.VMEM((2, 2) + half, bf16)
        spaces[f"plane{number}"] = pltpu.VMEM((2,) + half, bf16)
        spaces[f"line{number}"] = pltpu.VMEM((2, 2) + half, bf16)
        spaces[f"total{number}"] = pltpu.VMEM((2,) + half, bf16)
    dma = pltpu.SemaphoreType.DMA
    spaces.update(
        own_sem=dma((5,)),
        result_sem=dma((5,)),
        weight_send=dma((5, 9)),
        weight_recv=dma((5, 9)),
        gain_send=dma((GROUP,)),
        gain_recv=dma((GROUP,)),
        key_send=dma((2,)),
        key_recv=dma((2,)),
        swap_send=dma((1,)),
        swap_recv=dma((1,)),
        chip_send=dma((5, 2)),
        chip_recv=dma((5, 2)),
        pair_send=dma((5, 2)),
        pair_recv=dma((5, 2)),
        plane_send=dma((5, 2)),
        plane_recv=dma((5, 2)),
        line_send=dma((5, 2)),
        line_recv=dma((5, 2, 2)),
        total_send=dma((5, 2, 2)),
        total_recv=dma((5, 2)),
        small_send=dma((GROUP,)),
        small_recv=dma((GROUP,)),
        reps_send=dma((reps,)),
        reps_recv=dma((reps,)),
    )
    return spaces


class Refs:
    def __init__(self, names, refs):
        self.__dict__.update(zip(names, refs))


def column_sum(x):
    return jnp.sum(x, axis=0, keepdims=True)


def row_mean(x):
    return jnp.mean(x, axis=-1, keepdims=True)


def layer_kernel(names, shapes, *refs):
    v = Refs(names, refs)
    rep, me, lane, lanes = place()
    reps = lax.axis_size("rep")
    here = lax.axis_index("fsdp")
    core, across, along = me % 2, (me // 2) % 2, me // 4
    rows, width = v.tokens.shape
    parity = here % 2
    weights = [v.w_qkv, v.w_out, v.w_gate, v.w_up, v.w_down]
    named = lambda name: [getattr(v, f"{name}{number}") for number in range(5)]
    whole, stage, chip, pair = named("whole"), named("stage"), named("chip"), named("pair")
    plane, line, total, result = named("plane"), named("line"), named("total"), named("grad")

    def device(member):
        return (rep, member * lanes + lane)

    def remote(src, dst, send, recv, where):
        return pltpu.make_async_remote_copy(
            src_ref=src,
            dst_ref=dst,
            send_sem=send,
            recv_sem=recv,
            device_id=where,
            device_id_type=MESH,
        )

    barrier = pltpu.get_barrier_semaphore()
    greeted = [device(me ^ step) for step in range(1, GROUP)]
    greeted += [(lax.rem(rep + step, reps), here) for step in range(1, reps)]
    if lanes > 1:
        greeted.append((rep, here ^ 1))
    for where in greeted:
        pl.semaphore_signal(barrier, inc=1, device_id=where, device_id_type=MESH)
    pl.semaphore_wait(barrier, len(greeted))

    def slot(number, member):
        height = shapes[number][0]
        return whole[number].at[pl.ds(pl.multiple_of(member * height, 16), height), :]

    def half_slot(number, member, half):
        height, cols = split_shape(number, shapes[number])
        start = pl.multiple_of(member * shapes[number][0], 16)
        if number in (OUT, DOWN):
            return whole[number].at[pl.ds(start + half * height, height), :]
        return whole[number].at[pl.ds(start, height), pl.ds(half * cols, cols)]

    def weight_copy(number, kind):
        beside, ahead = me ^ ACROSS, me ^ ALONG
        if kind < 3:
            where = me ^ (CORE, ACROSS, ALONG)[kind]
            src, dst = weights[number], slot(number, me)
        else:
            src = (
                half_slot(number, beside, 0),
                half_slot(number, ahead, 1),
                slot(number, beside),
                slot(number, ahead),
                half_slot(number, beside ^ ALONG, 0),
                half_slot(number, beside ^ ALONG, 1),
            )[kind - 3]
            dst = src
            where = (ahead, beside)[kind - 3] if kind < 5 else me ^ CORE
        return remote(
            src,
            dst,
            v.weight_send.at[number, kind],
            v.weight_recv.at[number, kind],
            device(where),
        )

    def own_copy(number):
        return pltpu.make_async_copy(weights[number], slot(number, me), v.own_sem.at[number])

    def weight_begin(number):
        for kind in (1, 2, 0):
            weight_copy(number, kind).start()
        own_copy(number).start()

    def weight_forward(number):
        weight_copy(number, 1).wait_recv()
        weight_copy(number, 3).start()
        weight_copy(number, 5).start()
        weight_copy(number, 2).wait_recv()
        weight_copy(number, 4).start()
        weight_copy(number, 6).start()

    def weight_corner(number):
        weight_copy(number, 3).wait_recv()
        weight_copy(number, 7).start()
        weight_copy(number, 4).wait_recv()
        weight_copy(number, 8).start()

    def weight_ready(number):
        own_copy(number).wait()
        for kind in (0, 5, 6, 7, 8):
            weight_copy(number, kind).wait_recv()

    weight_begin(QKV)
    weight_begin(OUT)

    def gain_copy(step):
        return remote(
            v.gain_parts.at[me],
            v.gain_parts.at[me],
            v.gain_send.at[step],
            v.gain_recv.at[step],
            device(me ^ step),
        )

    v.gain_parts[me] = v.gain_part[...]
    for step in range(1, GROUP):
        gain_copy(step).start()
    weight_begin(GATE)
    v.squares[...] = jnp.zeros_like(v.squares)
    v.d_gains[...] = jnp.zeros_like(v.d_gains)
    v.d_key[...] = jnp.zeros_like(v.d_key)
    v.d_value[...] = jnp.zeros_like(v.d_value)
    for step in range(1, GROUP):
        gain_copy(step).wait_recv()
    v.gains[...] = jnp.sum(v.gain_parts[...], axis=0)

    prefix = v.prefix[0]

    def valid_rows(start, count):
        spot = lax.broadcasted_iota(jnp.int32, (count, 1), 0) + (parity * rows + start)
        return jnp.where(spot >= prefix, 1.0, 0.0)

    def by_rows(body):
        @pl.loop(0, rows // CHUNK)
        def _(k):
            start = pl.multiple_of(k * CHUNK, CHUNK)
            body(pl.ds(start, CHUNK), start)

    def by_columns(count, body):
        @pl.loop(0, count // TILE)
        def _(k):
            body(pl.ds(pl.multiple_of(k * TILE, TILE), TILE), k)

    def inverse_root(x):
        return lax.rsqrt(row_mean(x * x) + norm_epsilon)

    def norm_back(x, scale, upstream, gain, row):
        v.d_gains[row : row + 1, :] += column_sum(upstream * x * scale)
        spread = upstream * gain
        return scale * spread - x * (scale * scale * scale * row_mean(x * spread))

    gain_row = lambda k: v.gains[k : k + 1, :]

    def first_norm(here_rows, start):
        x = v.tokens[here_rows, :].astype(f32)
        normed = x * inverse_root(x) * gain_row(0)
        v.normed[here_rows, :] = normed.astype(bf16)
        v.one_t[:, here_rows] = normed.T.astype(bf16)
        v.squares[0:1, :] += column_sum(valid_rows(start, CHUNK) * (x * x))

    by_rows(first_norm)
    weight_forward(QKV)
    weight_corner(QKV)
    weight_ready(QKV)

    feats = HEADS * HEAD_DIM
    half_dim = HEAD_DIM // 2
    own_rows = pl.ds(pl.multiple_of(parity * rows, rows), rows)
    other_rows = pl.ds(pl.multiple_of((1 - parity) * rows, rows), rows)

    def rotate(x, sign):
        first, second = x[:, :half_dim], x[:, half_dim:]
        cosine, sine = v.cosine[...], v.sine[...] * sign
        return first * cosine - second * sine, second * cosine + first * sine

    def key_copy(number):
        ref = (v.key, v.value)[number]
        return remote(
            ref.at[own_rows, :],
            ref.at[own_rows, :],
            v.key_send.at[number],
            v.key_recv.at[number],
            (rep, here ^ 1),
        )

    key_part = dot(v.normed[...], whole[QKV][:, feats : feats + HEAD_DIM])
    first, second = rotate(key_part, 1.0)
    v.key[own_rows, :half_dim] = first.astype(bf16)
    v.key[own_rows, half_dim:] = second.astype(bf16)
    key_copy(0).start()
    v.value[own_rows, :] = dot(v.normed[...], whole[QKV][:, feats + HEAD_DIM :]).astype(bf16)
    key_copy(1).start()

    @pl.loop(0, HEADS)
    def _(head):
        start = pl.multiple_of(head * HEAD_DIM, HEAD_DIM)
        part = dot(v.normed[...], whole[QKV][:, pl.ds(start, HEAD_DIM)])
        first, second = rotate(part, 1.0)
        v.proj[:, pl.ds(start, half_dim)] = first.astype(bf16)
        v.proj[:, pl.ds(start + half_dim, half_dim)] = second.astype(bf16)

    weight_forward(OUT)
    weight_begin(UP)
    for number in range(2):
        key_copy(number).wait_recv()
    v.key_t[...] = v.key[...].astype(f32).T.astype(bf16)
    v.value_t[...] = v.value[...].astype(f32).T.astype(bf16)

    keys = v.key.shape[0]
    bend_scale = HEAD_DIM ** (-0.5) / soft_cap

    def scores(head, start):
        here_rows = pl.ds(start, TILE)
        query = v.proj[here_rows, head * HEAD_DIM : (head + 1) * HEAD_DIM]
        bent = jnp.tanh(dot_nt(v.key[...], query) * bend_scale)
        spot = lax.broadcasted_iota(jnp.int32, (1, TILE), 1) + (parity * rows + start)
        last = jnp.maximum(spot, prefix - 1)
        allowed = lax.broadcasted_iota(jnp.int32, (keys, TILE), 0) <= last
        return bent, jnp.where(allowed, jnp.exp(soft_cap * bent), 0.0), query

    def attend(head):
        cols = slice(head * HEAD_DIM, (head + 1) * HEAD_DIM)

        @pl.loop(0, rows // TILE)
        def _(k):
            start = pl.multiple_of(k * TILE, TILE)
            here_rows = pl.ds(start, TILE)
            _, power, _ = scores(head, start)
            inverse = 1.0 / column_sum(power)
            v.inverse[head : head + 1, here_rows] = inverse
            mixed = dot(v.value_t[...], (power * inverse).astype(bf16))
            v.att_t[cols, here_rows] = mixed.astype(bf16)
            v.att[here_rows, cols] = mixed.T.astype(bf16)

    attend(0)
    weight_corner(OUT)
    weight_forward(GATE)
    weight_begin(DOWN)
    attend(1)
    attend(2)
    weight_corner(GATE)
    weight_forward(UP)
    attend(3)
    weight_ready(OUT)

    v.branch[...] = dot(v.att[...], whole[OUT][...])

    def second_norm(here_rows, start):
        x = v.branch[here_rows, :]
        first_out = x * inverse_root(x) * gain_row(1)
        hidden = v.tokens[here_rows, :].astype(f32) + first_out
        v.hidden[here_rows, :] = hidden
        normed = hidden * inverse_root(hidden) * gain_row(2)
        v.normed[here_rows, :] = normed.astype(bf16)
        v.two_t[:, here_rows] = normed.T.astype(bf16)
        v.squares[1:2, :] += column_sum(valid_rows(start, CHUNK) * (first_out * first_out))

    by_rows(second_norm)
    weight_ready(GATE)
    weight_corner(UP)
    weight_ready(UP)
    weight_forward(DOWN)
    inner = shapes[GATE][1]

    def feed(cols, k):
        gate = dot(v.normed[...], whole[GATE][:, cols])
        upward = dot(v.normed[...], whole[UP][:, cols])
        square = gate * gate
        bent = jnp.tanh(0.7978845608028654 * (gate + 0.044715 * gate * square))
        open_half = 0.5 * (1.0 + bent)
        smooth = gate * open_half
        steep = open_half + gate * (1.0 - bent * bent) * (
            0.3989422804014327 * (1.0 + 3.0 * 0.044715 * square)
        )
        v.active[:, cols] = (smooth * upward).astype(bf16)
        v.bend[:, cols] = smooth.astype(bf16)
        v.slope[:, cols] = (steep * upward).astype(bf16)

    by_columns(inner, feed)
    weight_corner(DOWN)
    weight_ready(DOWN)

    v.d_tokens[...] = dot(v.active[...], whole[DOWN][...])

    def last_norm(here_rows, start):
        x = v.d_tokens[here_rows, :]
        scale = inverse_root(x)
        second_out = x * scale * gain_row(3)
        final = v.hidden[here_rows, :] + second_out
        v.output[here_rows, :] = final
        valid = valid_rows(start, CHUNK)
        v.squares[2:3, :] += column_sum(valid * (second_out * second_out))
        v.squares[3:4, :] += column_sum(valid * (final * final))
        upstream = v.cotangent[here_rows, :].astype(f32)
        v.normed[here_rows, :] = norm_back(x, scale, upstream, gain_row(3), 3).astype(bf16)

    by_rows(last_norm)

    def first_across(number, half):
        return any(one == (number, half) for one, _ in PAIRS)

    def chip_copy(number, half):
        return remote(
            stage[number].at[half, :, :, 1 - core],
            chip[number].at[half],
            v.chip_send.at[number, half],
            v.chip_recv.at[number, half],
            device(me ^ CORE),
        )

    def pair_copy(number, half):
        if first_across(number, half):
            src, where = chip[number].at[half, :, 1 - across], me ^ ACROSS
        else:
            src, where = chip[number].at[half, 1 - along], me ^ ALONG
        return remote(
            src,
            pair[number].at[half],
            v.pair_send.at[number, half],
            v.pair_recv.at[number, half],
            device(where),
        )

    def plane_copy(number, half):
        if first_across(number, half):
            src, where = pair[number].at[half, 1 - along], me ^ ALONG
        else:
            src, where = pair[number].at[half, 1 - across], me ^ ACROSS
        return remote(
            src,
            plane[number].at[half],
            v.plane_send.at[number, half],
            v.plane_recv.at[number, half],
            device(where),
        )

    def added(one, two):
        return (one.astype(f32) + two.astype(f32)).astype(bf16)

    def chip_begin(number, half):
        chip_copy(number, half).start()

    def chip_end(number, half):
        chip_copy(number, half).wait_recv()

        @pl.loop(0, 4)
        def _(k):
            one, two = k // 2, k % 2
            chip[number][half, one, two] = added(
                chip[number][half, one, two], stage[number][half, one, two, core]
            )

        pair_copy(number, half).start()

    def pair_end(number, half):
        pair_copy(number, half).wait_recv()

        @pl.loop(0, 2)
        def _(k):
            if first_across(number, half):
                mine = chip[number][half, k, across]
            else:
                mine = chip[number][half, along, k]
            pair[number][half, k] = added(pair[number][half, k], mine)

        plane_copy(number, half).start()

    def plane_end(number, half):
        plane_copy(number, half).wait_recv()
        kept = along if first_across(number, half) else across
        plane[number][half] = added(plane[number][half], pair[number][half, kept])

    order = [half for both in PAIRS for half in both]

    def sum_owner(number, half):
        return order.index((number, half)) % reps

    def line_copy(number, half):
        owner = sum_owner(number, half)
        side = jnp.where(rep < owner, 0, 1)
        return remote(
            plane[number].at[half],
            line[number].at[half, side],
            v.line_send.at[number, half],
            v.line_recv.at[number, half, side],
            (rep + 1 - 2 * side, here),
        )

    def line_wait(number, half, side):
        remote(
            plane[number].at[half],
            line[number].at[half, side],
            v.line_send.at[number, half],
            v.line_recv.at[number, half, side],
            (lax.rem(rep + 1, reps), here),
        ).wait_recv()

    inside = (rep > 0) & (rep < reps - 1)

    def line_begin(number, half):
        owner = sum_owner(number, half)

        @pl.when(rep != owner)
        def _():
            side = jnp.where(rep < owner, 0, 1)

            @pl.when(inside)
            def _():
                line_wait(number, half, side)
                plane[number][half] = added(plane[number][half], line[number][half, side])

            line_copy(number, half).start()

    def total_copy(number, half, way, step):
        return remote(
            total[number].at[half],
            total[number].at[half],
            v.total_send.at[number, half, way],
            v.total_recv.at[number, half],
            (rep + step, here),
        )

    def owner_ways(owner):
        return [w for w, there in ((0, owner > 0), (1, owner < reps - 1)) if there]

    def line_end(number, half):
        owner = sum_owner(number, half)

        @pl.when(rep == owner)
        def _():
            summed = plane[number][half].astype(f32)
            for side in owner_ways(owner):
                line_wait(number, half, side)
                summed = summed + line[number][half, side].astype(f32)
            total[number][half] = summed.astype(bf16)
            for way in owner_ways(owner):
                total_copy(number, half, way, 2 * way - 1).start()

    def total_end(number, half):
        owner = sum_owner(number, half)

        @pl.when(rep != owner)
        def _():
            away = jnp.where(rep < owner, -1, 1)
            total_copy(number, half, 0, away).wait_recv()

            @pl.when(inside)
            def _():
                total_copy(number, half, 0, away).start()

    def for_pair(action, index):
        for number, half in PAIRS[index]:
            action(number, half)

    def keep_columns(number, col_half, col, found):
        height = shapes[number][0]
        for member in range(GROUP):
            stage[number][
                col_half, member // 4, (member // 2) % 2, member % 2, :, pl.ds(col, TILE)
            ] = found[member * height : (member + 1) * height].astype(bf16)

    down_rows = shapes[DOWN][0]
    halved = inner // 2 // TILE

    def feed_back(side):
        @pl.loop(0, halved)
        def _(k):
            col = pl.multiple_of(k * TILE, TILE)
            start = pl.multiple_of(side * (inner // 2) + k * TILE, TILE)
            cols = pl.ds(start, TILE)
            d_active = dot_nt(v.normed[...], whole[DOWN][cols, :])
            d_gate = (d_active * v.slope[:, cols].astype(f32)).astype(bf16)
            d_upward = (d_active * v.bend[:, cols].astype(f32)).astype(bf16)
            v.slope[:, cols] = d_gate
            v.bend[:, cols] = d_upward
            keep_columns(GATE, side, col, dot(v.two_t[...], d_gate))
            keep_columns(UP, side, col, dot(v.two_t[...], d_upward))
            found = dot_tn(v.active[:, cols], v.normed[...]).astype(bf16)
            per = TILE // down_rows
            for part in range(per):
                member = (side * halved + k) * per + part
                y, x, c = member // 4, (member // 2) % 2, member % 2
                base = part * down_rows
                stage[DOWN][0, y, x, c] = found[base : base + down_rows // 2]
                stage[DOWN][1, y, x, c] = found[base + down_rows // 2 : base + down_rows]

    feed_back(0)
    for_pair(chip_begin, 0)
    feed_back(1)
    for_pair(chip_begin, 1)
    for_pair(chip_begin, 2)
    for_pair(chip_end, 0)
    v.d_tokens[...] = dot_nt(v.slope[...], whole[GATE][...]) + dot_nt(
        v.bend[...], whole[UP][...]
    )
    for_pair(chip_end, 1)

    def middle_norms(here_rows, start):
        x = v.hidden[here_rows, :]
        flow = norm_back(x, inverse_root(x), v.d_tokens[here_rows, :], gain_row(2), 2)
        d_hidden = v.cotangent[here_rows, :].astype(f32) + flow
        v.d_tokens[here_rows, :] = d_hidden
        x = v.branch[here_rows, :]
        flow = norm_back(x, inverse_root(x), d_hidden, gain_row(1), 1)
        v.normed[here_rows, :] = flow.astype(bf16)

    by_rows(middle_norms)
    for_pair(chip_end, 2)
    out_rows = shapes[OUT][0]
    v.att[...] = dot_nt(v.normed[...], whole[OUT][...]).astype(bf16)

    @pl.loop(0, GROUP // 2)
    def _(k):
        start = pl.multiple_of(k * 2 * out_rows, 2 * out_rows)
        found = dot(v.att_t[pl.ds(start, 2 * out_rows), :], v.normed[...]).astype(bf16)
        for part in range(4):
            stage[OUT][part % 2, k // 2, k % 2, part // 2] = found[
                part * (out_rows // 2) : (part + 1) * (out_rows // 2)
            ]

    for_pair(chip_begin, 3)

    def attend_back(head):
        cols = slice(head * HEAD_DIM, (head + 1) * HEAD_DIM)

        @pl.loop(0, rows // TILE)
        def _(k):
            start = pl.multiple_of(k * TILE, TILE)
            here_rows = pl.ds(start, TILE)
            bent, power, query = scores(head, start)
            soft = power * v.inverse[head : head + 1, here_rows]
            flow = v.att[here_rows, cols]
            d_soft = dot_nt(v.value[...], flow)
            v.d_value[...] += dot(soft.astype(bf16), flow)
            level = column_sum(d_soft * soft)
            d_raw = soft * (d_soft - level) * ((1.0 - bent * bent) * HEAD_DIM ** (-0.5))
            d_raw = d_raw.astype(bf16)
            v.d_key[...] += dot(d_raw, query)
            d_query = dot(v.key_t[...], d_raw).T
            first, second = d_query[:, :half_dim], d_query[:, half_dim:]
            cosine, sine = v.cosine[here_rows, :], v.sine[here_rows, :]
            base = head * HEAD_DIM
            v.proj[here_rows, base : base + half_dim] = (first * cosine + second * sine).astype(
                bf16
            )
            v.proj[here_rows, base + half_dim : base + HEAD_DIM] = (
                second * cosine - first * sine
            ).astype(bf16)

    swap = remote(
        v.swap_out,
        v.swap_in,
        v.swap_send.at[0],
        v.swap_recv.at[0],
        (rep, here ^ 1),
    )

    attend_back(0)
    for_pair(chip_end, 3)
    for_pair(pair_end, 0)
    attend_back(1)
    for_pair(pair_end, 1)
    for_pair(plane_end, 0)
    for_pair(line_begin, 0)
    attend_back(2)
    for_pair(pair_end, 2)
    for_pair(plane_end, 1)
    for_pair(line_begin, 1)
    for_pair(line_end, 0)
    attend_back(3)
    v.swap_out[0] = v.d_key[other_rows, :].astype(bf16)
    v.swap_out[1] = v.d_value[other_rows, :].astype(bf16)
    swap.start()
    for_pair(pair_end, 3)
    for_pair(plane_end, 2)
    for_pair(line_begin, 2)
    for_pair(line_end, 1)
    for_pair(total_end, 0)

    qkv_half = split_shape(QKV, shapes[QKV])[1] // TILE

    def projection_grad(tile):
        found = dot(v.one_t[...], v.proj[:, tile * TILE : (tile + 1) * TILE])
        keep_columns(QKV, tile // qkv_half, (tile % qkv_half) * TILE, found)

    for tile in range(qkv_half):
        projection_grad(tile)
    chip_begin(QKV, 0)
    swap.wait_recv()
    d_key = v.d_key[own_rows, :] + v.swap_in[0].astype(f32)
    first, second = rotate(d_key, -1.0)
    v.proj[:, feats : feats + half_dim] = first.astype(bf16)
    v.proj[:, feats + half_dim : feats + HEAD_DIM] = second.astype(bf16)
    v.proj[:, feats + HEAD_DIM :] = (
        v.d_value[own_rows, :] + v.swap_in[1].astype(f32)
    ).astype(bf16)
    for tile in range(qkv_half, 2 * qkv_half):
        projection_grad(tile)
    chip_begin(QKV, 1)
    for_pair(chip_end, 4)
    v.branch[...] = dot_nt(v.proj[...], whole[QKV][...])

    def first_norm_back(here_rows, start):
        x = v.tokens[here_rows, :].astype(f32)
        flow = norm_back(x, inverse_root(x), v.branch[here_rows, :], gain_row(0), 0)
        v.d_tokens[here_rows, :] += flow

    by_rows(first_norm_back)

    def small_copy(step):
        return remote(
            v.small_parts.at[me],
            v.small_parts.at[me],
            v.small_send.at[step],
            v.small_recv.at[step],
            device(me ^ step),
        )

    def reps_copy(step):
        return remote(
            v.small_reps.at[rep],
            v.small_reps.at[rep],
            v.reps_send.at[step],
            v.reps_recv.at[step],
            (lax.rem(rep + step, reps), here),
        )

    spot = lax.broadcasted_iota(jnp.int32, (1, width), 1)
    numbers = jnp.where(spot == 4, column_sum(valid_rows(0, rows)), 0.0)
    for k in range(4):
        summed = jnp.sum(v.squares[k : k + 1, :], axis=1, keepdims=True)
        numbers = numbers + jnp.where(spot == k, summed, 0.0)
    v.d_gains[4:5, :] = numbers
    v.small_parts[me] = v.d_gains[...]
    for step in range(1, GROUP):
        small_copy(step).start()
    for_pair(pair_end, 4)
    for_pair(plane_end, 3)
    for_pair(line_begin, 3)
    for_pair(line_end, 2)
    for_pair(total_end, 1)
    for step in range(1, GROUP):
        small_copy(step).wait_recv()
    v.small_reps[rep] = jnp.sum(v.small_parts[...], axis=0)
    for step in range(1, reps):
        reps_copy(step).start()
    for_pair(plane_end, 4)
    for_pair(line_begin, 4)
    for_pair(line_end, 3)
    for_pair(total_end, 2)
    for_pair(line_end, 4)
    for_pair(total_end, 3)
    for_pair(total_end, 4)
    for step in range(1, reps):
        reps_copy(step).wait_recv()
    v.small[...] = jnp.sum(v.small_reps[...], axis=0)
    results = [
        pltpu.make_async_copy(total[number], result[number], v.result_sem.at[number])
        for number in range(5)
    ]
    for copy in results:
        copy.start()

    for number in range(5):
        for kind in range(9):
            weight_copy(number, kind).wait_send()
    for number in range(2):
        key_copy(number).wait_send()
    swap.wait_send()
    for step in range(1, GROUP):
        gain_copy(step).wait_send()
        small_copy(step).wait_send()
    for step in range(1, reps):
        reps_copy(step).wait_send()
    for number, half in order:
        chip_copy(number, half).wait_send()
        pair_copy(number, half).wait_send()
        plane_copy(number, half).wait_send()
        owner = sum_owner(number, half)

        @pl.when(rep != owner)
        def _():
            line_copy(number, half).wait_send()

            @pl.when(inside)
            def _():
                total_copy(number, half, 0, jnp.where(rep < owner, -1, 1)).wait_send()

        @pl.when(rep == owner)
        def _():
            for way in owner_ways(owner):
                total_copy(number, half, way, 2 * way - 1).wait_send()

    for copy in results:
        copy.wait()


def layer(prefix, tokens, cotangent, cosine, sine, gain_part, weights, reps):
    shapes = tuple(w.shape for w in weights)
    rows, width = tokens.shape
    spaces = layer_names(rows, 2 * rows, width, shapes, reps)
    halves = [split_shape(number, shape) for number, shape in enumerate(shapes)]
    inputs = ["prefix", "tokens", "cotangent", "cosine", "sine", "gain_part"]
    inputs += ["w_qkv", "w_out", "w_gate", "w_up", "w_down"]
    outputs = ["output", "d_tokens", "small"] + [f"grad{number}" for number in range(5)]
    vmem = pl.BlockSpec(memory_space=pltpu.VMEM)
    names = inputs + outputs + list(spaces)
    out = pl.pallas_call(
        lambda *refs: layer_kernel(names, shapes, *refs),
        out_shape=[
            jax.ShapeDtypeStruct((rows, width), f32),
            jax.ShapeDtypeStruct((rows, width), f32),
            jax.ShapeDtypeStruct((8, width), f32),
        ]
        + [jax.ShapeDtypeStruct((2,) + half, bf16) for half in halves],
        in_specs=[pl.BlockSpec(memory_space=pltpu.SMEM)]
        + [vmem] * 5
        + [pl.BlockSpec(memory_space=pl.ANY)] * 5,
        out_specs=[vmem] * 3 + [pl.BlockSpec(memory_space=pl.ANY)] * 5,
        scratch_shapes=list(spaces.values()),
        compiler_params=pltpu.CompilerParams(
            collective_id=2, has_side_effects=True, vmem_limit_bytes=64 * 2**20
        ),
        name="layer",
    )(prefix, tokens, cotangent, cosine, sine, gain_part, *weights)
    return out[0], out[1], out[2], out[3:]


OWNERS = (6, 7, 0, 2, 4)
FLIPPED = (False, True, False, False, True)


def gram_into(x_ref, gram):
    rows = gram.shape[0]
    starts = list(range(0, rows, 256))
    for j in starts:
        n = min(256, rows - j)
        gram[j:rows, j : j + n] = dot_nt(x_ref[j:rows, :], x_ref[j : j + n, :])
    for j in starts:
        n = min(256, rows - j)
        if j + n < rows:
            gram[j : j + n, j + n : rows] = gram[j + n : rows, j : j + n].T


def newton_step(x_ref, gram, mixer, high, low, first, refined):
    gram_into(x_ref, gram)
    rows = gram.shape[0]
    same = lax.broadcasted_iota(jnp.int32, (rows, rows), 0) == lax.broadcasted_iota(
        jnp.int32, (rows, rows), 1
    )
    whole = gram[...]
    scale = None
    if first:
        scale = 1.0 / (jnp.sqrt(jnp.sum(jnp.where(same, whole, 0.0))) + frobenius_epsilon)
        whole = whole * (scale * scale)
        gram[...] = whole
    high[...] = whole.astype(bf16)
    squared = dot(high[...], high[...])
    if refined:
        low[...] = (gram[...] - high[...].astype(f32)).astype(bf16)
        squared = squared + dot(high[...], low[...]) + dot(low[...], high[...])
    mix = (
        jnp.where(same, newton_first, 0.0) + newton_second * gram[...] + newton_third * squared
    )
    if first:
        mix = mix * scale
    mixer[...] = mix.astype(bf16)
    width = x_ref.shape[1]
    tile = 1024 if width % 1024 == 0 else width

    @pl.loop(0, width // tile)
    def _(t):
        cols = pl.ds(pl.multiple_of(t * tile, tile), tile)
        x_ref[:, cols] = dot(mixer[...], x_ref[:, cols]).astype(bf16)


def muon_kernel(shapes, *refs):
    grads, moments, results = refs[0:5], refs[5:10], refs[10:15]
    outgoing, arrived = refs[15:20], refs[20:25]
    x_all, gram, mixer, high, low = refs[25:30]
    gather_send, gather_recv, scatter_send, scatter_recv = refs[30:34]
    rep, me, lane, lanes = place()

    def device(member):
        return (rep, member * lanes + lane)

    owner_here = me == OWNERS[0]
    for owner in OWNERS[1:]:
        owner_here = owner_here | (me == owner)

    @pl.when(owner_here)
    def _():
        x_all[...] = jnp.zeros_like(x_all)

    barrier = pltpu.get_barrier_semaphore()
    for step in range(1, GROUP):
        pl.semaphore_signal(
            barrier, inc=1, device_id=device(me ^ step), device_id_type=MESH
        )

    def block(number, member):
        rows, cols = shapes[number]
        if FLIPPED[number]:
            return x_all.at[:, pl.ds(member * rows, rows)]
        return x_all.at[pl.ds(member * rows, rows), pl.ds(0, cols)]

    for number in range(5):
        grad = jnp.concatenate(
            [grads[number][0], grads[number][1]], axis=0 if number in (OUT, DOWN) else 1
        ).astype(f32)
        new = momentum_decay * moments[number][...] + (1.0 - momentum_decay) * grad
        nesterov = (1.0 - momentum_decay) * grad + momentum_decay * new
        if FLIPPED[number]:
            nesterov = nesterov.T
        outgoing[number][...] = nesterov.astype(bf16)
    pl.semaphore_wait(barrier, GROUP - 1)

    def gather_copy(number, member, sender):
        rows, _ = shapes[number]
        if FLIPPED[number]:
            start = pl.multiple_of(sender * rows, rows)
            target = x_all.at[:, pl.ds(start, rows)]
        else:
            start = pl.multiple_of(sender * rows, 16)
            target = x_all.at[pl.ds(start, rows), pl.ds(0, shapes[number][1])]
        return pltpu.make_async_remote_copy(
            src_ref=outgoing[number],
            dst_ref=target,
            send_sem=gather_send.at[number],
            recv_sem=gather_recv.at[sender],
            device_id=device(member),
            device_id_type=MESH,
        )

    for number in (2, 3, 4, 0, 1):

        @pl.when(me != OWNERS[number])
        def _():
            gather_copy(number, OWNERS[number], me).start()

    for number in range(5):
        owner = OWNERS[number]

        @pl.when(me == owner)
        def _():
            rows, cols = shapes[number]
            if FLIPPED[number]:
                x_all[:, owner * rows : (owner + 1) * rows] = outgoing[number][...]
            else:
                x_all[owner * rows : (owner + 1) * rows, 0:cols] = outgoing[number][...]
            for step in range(1, GROUP):
                gather_copy(number, owner, owner ^ step).wait_recv()

    @pl.when(owner_here)
    def _():
        newton_step(x_all, gram, mixer, high, low, True, False)

        @pl.loop(0, NS_STEPS - 3)
        def _(k):
            newton_step(x_all, gram, mixer, high, low, False, False)

        @pl.loop(0, 2)
        def _(k):
            newton_step(x_all, gram, mixer, high, low, False, True)

    def scatter_copy(number, member):
        rows, cols = shapes[number]
        return pltpu.make_async_remote_copy(
            src_ref=block(number, member),
            dst_ref=arrived[number],
            send_sem=scatter_send.at[member],
            recv_sem=scatter_recv.at[number],
            device_id=device(member),
            device_id_type=MESH,
        )

    for number in range(5):
        owner = OWNERS[number]

        @pl.when(me == owner)
        def _():
            for step in range(1, GROUP):
                scatter_copy(number, owner ^ step).start()
            arrived[number][...] = block(number, owner)[...]

    for number in range(5):
        owner = OWNERS[number]

        @pl.when(me != owner)
        def _():
            scatter_copy(number, owner).wait_recv()

        update = arrived[number][...]
        if FLIPPED[number]:
            update = update.astype(f32).T.astype(bf16)
        results[number][...] = update

    for number in range(5):
        owner = OWNERS[number]

        @pl.when(me == owner)
        def _():
            for step in range(1, GROUP):
                scatter_copy(number, owner ^ step).wait_send()

        @pl.when(me != owner)
        def _():
            gather_copy(number, owner, me).wait_send()


def muon(grads, moments):
    shapes = tuple(moment.shape for moment in moments)
    flipped = [s[::-1] if flip else s for s, flip in zip(shapes, FLIPPED)]
    side = shapes[0][0] * GROUP
    width = max(s[0] * GROUP if flip else s[1] for s, flip in zip(shapes, FLIPPED))
    vmem = pl.BlockSpec(memory_space=pltpu.VMEM)
    return pl.pallas_call(
        lambda *refs: muon_kernel(shapes, *refs),
        out_shape=[jax.ShapeDtypeStruct(s, bf16) for s in shapes],
        in_specs=[vmem] * 10,
        out_specs=[vmem] * 5,
        scratch_shapes=[pltpu.VMEM(s, bf16) for s in flipped]
        + [pltpu.VMEM(s, bf16) for s in flipped]
        + [
            pltpu.VMEM((side, width), bf16),
            pltpu.VMEM((side, side), f32),
            pltpu.VMEM((side, side), bf16),
            pltpu.VMEM((side, side), bf16),
            pltpu.VMEM((side, side), bf16),
            pltpu.SemaphoreType.DMA((5,)),
            pltpu.SemaphoreType.DMA((GROUP,)),
            pltpu.SemaphoreType.DMA((GROUP,)),
            pltpu.SemaphoreType.DMA((5,)),
        ],
        compiler_params=pltpu.CompilerParams(
            collective_id=1, has_side_effects=True, vmem_limit_bytes=48 * 2**20
        ),
        name="muon",
    )(*grads, *moments)


def finish_kernel(factors, *refs):
    grads, updates, moments, weights = refs[0:5], refs[5:10], refs[10:15], refs[15:20]
    streams = refs[20:22]
    wide, news, masters = refs[22:27], refs[27:32], refs[32:37]
    for number in range(5):
        grad = grads[number][0].astype(f32)
        wide[number][...] = grad
        news[number][...] = (
            momentum_decay * moments[number][...] + (1.0 - momentum_decay) * grad
        )
        masters[number][...] = weights[number][...].astype(f32) - factors[number] * updates[
            number
        ][...].astype(f32)
    for source, target in zip(streams, refs[37:39]):
        target[...] = source[...]


def finish(grads, updates, moments, weights, streams):
    steps = 4
    shapes = tuple(moment.shape for moment in moments)
    factors = [max(1.0, s[0] * GROUP / s[1]) ** 0.5 * muon_rate for s in shapes]
    halves, wholes = [], []
    for number, (rows, cols) in enumerate(shapes):
        if number in (OUT, DOWN):
            halves.append(pl.BlockSpec((1, rows // steps, cols), lambda j: (j // 2, j % 2, 0)))
            wholes.append(pl.BlockSpec((rows // steps, cols), lambda j: (j, 0)))
        else:
            halves.append(pl.BlockSpec((1, rows, cols // steps), lambda j: (j // 2, 0, j % 2)))
            wholes.append(pl.BlockSpec((rows, cols // steps), lambda j: (0, j)))
    lines = [
        pl.BlockSpec((s.shape[0] // steps, s.shape[1]), lambda j: (j, 0)) for s in streams
    ]
    out = pl.pallas_call(
        lambda *refs: finish_kernel(factors, *refs),
        grid=(steps,),
        out_shape=[jax.ShapeDtypeStruct(s, f32) for s in shapes * 3]
        + [jax.ShapeDtypeStruct(s.shape, f32) for s in streams],
        in_specs=halves + wholes * 3 + lines,
        out_specs=wholes * 3 + lines,
        compiler_params=pltpu.CompilerParams(vmem_limit_bytes=48 * 2**20),
        name="finish",
    )(*grads, *updates, *moments, *weights, *streams)
    return out[0:5], out[5:10], out[10:15], out[15:17]


def shards(
    tokens,
    cotangent,
    prefix,
    w_qkv,
    w_out,
    w_gate,
    w_up,
    w_down,
    gains,
    moment_qkv,
    moment_out,
    moment_gate,
    moment_up,
    moment_down,
    gain_first,
    gain_second,
):
    rows, width = tokens.shape
    reps = lax.axis_size("rep")
    here = lax.axis_index("fsdp")
    rep, me, lane, lanes = place()
    teams = [[member * lanes + k for k in range(lanes)] for member in range(GROUP)]

    def joined(shard):
        if lanes == 1:
            return shard
        return lax.all_gather(shard, "fsdp", axis=0, tiled=True, axis_index_groups=teams)

    def summed(term):
        if lanes == 1:
            return term
        parts = lax.all_gather(term, "fsdp", axis_index_groups=teams)
        return jnp.sum(parts.astype(f32), axis=0).astype(term.dtype)

    def parted(block):
        if lanes == 1:
            return block
        size = block.shape[0] // lanes
        return lax.dynamic_slice_in_dim(block, lane * size, size, 0)

    sequence_id = (rep * lax.axis_size("fsdp") + here) // 2
    prefix_len = lax.dynamic_slice_in_dim(prefix, sequence_id, 1, 0)
    positions = here % 2 * rows + jnp.arange(rows, dtype=jnp.int32)
    cosine, sine = rotary_tables(positions, HEAD_DIM)
    gain_block = joined(gains).astype(f32).T
    gain_part = lax.dynamic_update_slice(
        jnp.zeros((8, width), f32), gain_block, (0, me * gain_block.shape[1])
    )
    weights = [joined(term) for term in (w_qkv, w_out, w_gate, w_up, w_down)]
    moments = [
        joined(term)
        for term in (moment_qkv, moment_out, moment_gate, moment_up, moment_down)
    ]
    output, d_tokens, small, halves = layer(
        prefix_len, tokens, cotangent, cosine, sine, gain_part, weights, reps
    )
    halves = [summed(term) for term in halves]
    small = summed(small)
    updates = muon(halves, moments)
    grads, news, masters, streams = finish(
        halves, updates, moments, weights, (output, d_tokens)
    )
    grads, news, masters = (
        [parted(term) for term in group] for group in (grads, news, masters)
    )
    statistics = jnp.sqrt(small[4, 0:4] / (small[4, 4] * width))
    count = gains.shape[0]
    gain_grad = lax.dynamic_slice(small, (0, here * count), (4, count)).T
    gains_local = gains.astype(f32)
    first_new = first_decay * gain_first + (1.0 - first_decay) * gain_grad
    second_new = second_decay * gain_second + (1.0 - second_decay) * gain_grad * gain_grad
    first_hat = first_new / (1.0 - first_decay**ADAM_STEP)
    second_hat = second_new / (1.0 - second_decay**ADAM_STEP)
    master_gains = gains_local - adam_rate * (
        first_hat / (jnp.sqrt(second_hat) + adam_epsilon) + weight_decay * gains_local
    )
    return (
        *streams,
        *grads,
        gain_grad,
        *news,
        *masters,
        first_new,
        second_new,
        master_gains,
        statistics,
    )


def solution(mesh):
    in_specs = (
        P(("rep", "fsdp"), None),
        P(("rep", "fsdp"), None),
        P(),
        P("fsdp", None),
        P("fsdp", None),
        P("fsdp", None),
        P("fsdp", None),
        P("fsdp", None),
        P("fsdp", None),
        P("fsdp", None),
        P("fsdp", None),
        P("fsdp", None),
        P("fsdp", None),
        P("fsdp", None),
        P("fsdp", None),
        P("fsdp", None),
    )
    out_specs = (
        P(("rep", "fsdp"), None),
        P(("rep", "fsdp"), None),
        P("fsdp", None),
        P("fsdp", None),
        P("fsdp", None),
        P("fsdp", None),
        P("fsdp", None),
        P("fsdp", None),
        P("fsdp", None),
        P("fsdp", None),
        P("fsdp", None),
        P("fsdp", None),
        P("fsdp", None),
        P("fsdp", None),
        P("fsdp", None),
        P("fsdp", None),
        P("fsdp", None),
        P("fsdp", None),
        P("fsdp", None),
        P("fsdp", None),
        P("fsdp", None),
        P(),
    )
    return jax.shard_map(shards, mesh=mesh, in_specs=in_specs, out_specs=out_specs, check_vma=False)
```

time: 705 us -> 306 us (0.43)
  the two profiles are of different devices: /device:TPU:0 before, /device:TPU:25 now
where the time goes in v2:
time: 306 us; the launch traced here: 302 us
  Pallas kernels  280 us (92%)
  local copies, waits for them, and re-layouts  15.7 us (5%)
  other arithmetic  5.14 us (2%)
    pallas_call x1, Pallas kernels, layer(): pl.pallas_call(lambda *refs: layer_kernel(names, shapes, *refs), out_shap...  203 us
    pallas_call x1, Pallas kernels, muon(): pl.pallas_call(lambda *refs: muon_kernel(shapes, *refs), out_shape=[jax.S...  69.9 us
    unnamed x46, local copies, waits for them, and re-layouts  11 us
    pallas_call x1, Pallas kernels, finish(): pl.pallas_call(lambda *refs: finish_kernel(factors, *refs), grid=(steps,)...  6.81 us

profile of v2, /device:TPU:25, one launch (start us, length us, event | category | flops | bytes accessed | tf_op | source)
XLA Modules:
  0.0 302.5 jit_solution(1136520873843241086)
XLA Ops:
  0.7 1.2 dynamic_slice.6.refs_0_
  1.9 0.7 convert_bitcast_fusion
  2.6 0.6 broadcast_in_dim.2
  3.2 1.6 dynamic_update_slice.3.refs_5_
  4.8 1.8 multiply_sine_fusion
  6.7 203.1 %layer.1 = (f32[512,640]{1,0:T(8,128)}, f32[512,640]{1,0:T(8,128)}, f32[8,640]{1,0:T(8,128)}, bf16[2,80,768]{2,1,0:T(8,128)(2,1)}, bf16[2,64,640]{2,1,0:T(8,128)...) custom-call(s32[1]{0:T(128)} %dynamic_slice.6.refs_0_, ...), custom_call_target="tpu_custom_call" | custom-call | tf_op jit(solution)/shard_map/layer/pallas_call | solution.py:866
  209.8 1.3 slice.7
  211.7 1.2 sqrt_bitcast_fusion
  212.9 1.4 convert_subtract_fusion
  214.4 0.0 copy-start
  214.4 1.1 copy-done
  215.4 0.0 copy-start.2
  215.4 1.1 copy-done.2
  216.5 0.0 copy-start.3
  216.5 1.1 copy-done.3
  217.6 0.0 copy-start.4
  217.6 1.0 copy-done.4
  218.6 0.0 copy-start.6
  218.6 1.0 copy-done.6
  219.6 1.0 copy-done.8
  220.6 1.0 copy-done.10
  221.6 1.0 copy-done.12
  222.5 0.9 copy-done.17
  223.5 0.9 copy-done.20
  224.4 0.0 copy-start.11
  224.4 0.0 copy-start.13
  224.4 0.0 copy-start.14
  224.4 0.0 copy-start.15
  224.5 0.0 copy-start.16
  224.5 0.0 copy-start.18
  224.5 0.0 copy-start.19
  224.5 0.0 copy-start.21
  224.5 69.9 %muon.1 = (bf16[80,1536]{1,0:T(8,128)(2,1)S(1)}, bf16[128,640]{1,0:T(8,128)(2,1)S(1)}, bf16[80,2048]{1,0:T(8,128)(2,1)S(1)}, bf16[80,2048]{1,0:T(8,128)(2,1)S(1)}, bf16[256,640]{1,0:T(8,128)(2,1)S(1)}) custom-call(bf16[2,80,768]{2,1,0:T(8,128)(2,1)S(1)} %copy-done.17, bf16[2,64,640]{2,1,0:T(8,128)(2,1)S(1)} %copy-done.20, ...), custom_call_target="tpu_custom_call" | custom-call | tf_op jit(solution)/shard_map/muon/pallas_call | solution.py:1075
  294.4 0.0 copy-done.1
  294.4 0.0 copy-done.5
  294.5 0.0 copy-done.7
  294.5 0.0 copy-done.9
  294.5 0.0 copy-done.11
  294.5 0.0 copy-done.13
  294.5 0.0 copy-done.14
  294.5 0.0 copy-done.15
  294.5 0.0 copy-done.16
  294.5 0.0 copy-done.18
  294.5 0.0 copy-done.19
  294.5 0.0 copy-done.21
  294.6 0.0 copy-start.22
  294.6 0.9 copy-done.22
  295.5 6.8 %finish.1 = (f32[80,1536]{1,0:T(8,128)}, f32[128,640]{1,0:T(8,128)}, f32[80,2048]{1,0:T(8,128)}, f32[80,2048]{1,0:T(8,128)}, f32[256,640]{1,0:T(8,128)}, /*index...) custom-call(bf16[2,80,768]{2,1,0:T(8,128)(2,1)S(1)} %copy-done.18, ...), custom_call_target="tpu_custom_call" | custom-call | tf_op jit(solution)/shard_map/finish/pallas_call | solution.py:1132
  (11 shorter events, 0.0 us)
Async XLA Ops:
  214.4 1.1 copy-start
  215.4 1.1 copy-start.2
  216.5 1.1 copy-start.3
  217.6 1.0 copy-start.4
  218.6 1.0 copy-start.6
  219.6 1.0 copy-start.8
  220.6 1.0 copy-start.10
  221.6 1.0 copy-start.12
  222.5 0.9 copy-start.17
  223.5 0.9 copy-start.20
  224.4 70.0 %copy-start.1 = (f32[80,2048]{1,0:T(8,128)S(1)}, f32[80,2048]{1,0:T(8,128)}, u32[]{:S(2)}) copy-start(f32[80,2048]{1,0:T(8,128)} %refs_12_.1) | copy-start | bytes 1966084
  224.4 70.0 %copy-start.5 = (f32[80,1536]{1,0:T(8,128)S(1)}, f32[80,1536]{1,0:T(8,128)}, u32[]{:S(2)}) copy-start(f32[80,1536]{1,0:T(8,128)} %refs_10_.3) | copy-start | bytes 1474564
  224.4 70.0 %copy-start.7 = (f32[128,640]{1,0:T(8,128)S(1)}, f32[128,640]{1,0:T(8,128)}, u32[]{:S(2)}) copy-start(f32[128,640]{1,0:T(8,128)} %refs_11_.1) | copy-start | bytes 983044
  224.4 70.1 %copy-start.9 = (bf16[2,80,1024]{2,1,0:T(8,128)(2,1)S(1)}, bf16[2,80,1024]{2,1,0:T(8,128)(2,1)}, u32[]{:S(2)}) copy-start(bf16[2,80,1024]{2,1,0:T(8,128)(2,1)} %get-tuple-element.54.refs_2_) | copy-start | bytes 983044
  224.4 70.1 %copy-start.11 = (bf16[2,80,1024]{2,1,0:T(8,128)(2,1)S(1)}, bf16[2,80,1024]{2,1,0:T(8,128)(2,1)}, u32[]{:S(2)}) copy-start(bf16[2,80,1024]{2,1,0:T(8,128)(2,1)} %get-tuple-element.55.refs_3_) | copy-start | bytes 983044
  224.4 70.1 %copy-start.13 = (bf16[2,128,640]{2,1,0:T(8,128)(2,1)S(1)}, bf16[2,128,640]{2,1,0:T(8,128)(2,1)}, u32[]{:S(2)}) copy-start(bf16[2,128,640]{2,1,0:T(8,128)(2,1)} %get-tuple-element.56.refs_4_) | copy-start | bytes 983044
  224.4 70.1 %copy-start.14 = (bf16[80,2048]{1,0:T(8,128)(2,1)S(1)}, bf16[80,2048]{1,0:T(8,128)(2,1)}, u32[]{:S(2)}) copy-start(bf16[80,2048]{1,0:T(8,128)(2,1)} %refs_17_.1) | copy-start | bytes 983044
  224.4 70.1 %copy-start.15 = (bf16[80,2048]{1,0:T(8,128)(2,1)S(1)}, bf16[80,2048]{1,0:T(8,128)(2,1)}, u32[]{:S(2)}) copy-start(bf16[80,2048]{1,0:T(8,128)(2,1)} %refs_18_.1) | copy-start | bytes 983044
  224.5 70.1 %copy-start.16 = (bf16[256,640]{1,0:T(8,128)(2,1)S(1)}, bf16[256,640]{1,0:T(8,128)(2,1)}, u32[]{:S(2)}) copy-start(bf16[256,640]{1,0:T(8,128)(2,1)} %refs_19_.1) | copy-start | bytes 983044
  224.5 70.1 %copy-start.18 = (bf16[2,80,768]{2,1,0:T(8,128)(2,1)S(1)}, bf16[2,80,768]{2,1,0:T(8,128)(2,1)}, u32[]{:S(2)}) copy-start(bf16[2,80,768]{2,1,0:T(8,128)(2,1)} %get-tuple-element.52.refs_0_) | copy-start | bytes 737284
  224.5 70.1 %copy-start.19 = (bf16[80,1536]{1,0:T(8,128)(2,1)S(1)}, bf16[80,1536]{1,0:T(8,128)(2,1)}, u32[]{:S(2)}) copy-start(bf16[80,1536]{1,0:T(8,128)(2,1)} %refs_15_.1) | copy-start | bytes 737284
  224.5 70.1 %copy-start.21 = (bf16[2,64,640]{2,1,0:T(8,128)(2,1)S(1)}, bf16[2,64,640]{2,1,0:T(8,128)(2,1)}, u32[]{:S(2)}) copy-start(bf16[2,64,640]{2,1,0:T(8,128)(2,1)} %get-tuple-element.53.refs_1_) | copy-start | bytes 491524
  294.6 0.9 copy-start.22
